TPU v7x, 256 devices: a whole 4x4x8 slice. The times are simulated.
256 devices in a mesh: rows: 32 (over x, z), cols: 8 (over y, core).
Axes of the slice: x: 4, y: 4, z: 8, core: 2. Of those that a mesh axis runs over, the one named last changes fastest.
Arguments:
- vectors: bfloat16 [65536, 768], P('rows'), may hold values from -24 to 24
- centroids: bfloat16 [8192, 768], P('cols'), may hold values from -0.2 to 0.2
Outputs:
- new_centroids: float32 [8192, 768], P('cols')
- row_potential: float32 [65536], P('rows')
- col_potential: float32 [8192], P('cols')
All inputs are finite; a program needn't handle non-finite values.
Results may differ from a plain program's by a relative error of at most 0.0023.
Values sent between devices are 32-bit elements; how exact they have to be, the bound alone decides.
No kernel may reach another device: no remote copies, remote signals or barrier semaphores. Data moves between devices by JAX's collectives and lax.ppermute only.
A program may use at most 64 MiB of HBM per device.

v0:
```python
import functools
import math

import jax
import jax.numpy as jnp
from jax import lax
from jax.experimental import pallas as pl
from jax.experimental.pallas import tpu as pltpu
from jax.sharding import PartitionSpec as P

ITERS = 3
LANES = 128
LIM = 40.0
MIB = 1024 * 1024
F32 = jnp.float32
LOG2E = math.log2(math.e)
XS, ZS = 4, 8
BLOCK = 32
PARTS = BLOCK // 8
CHUNKS = 4
XB1, XB2, ZB1, ZB2 = range(4)


def combine_lse(parts):
    top = jnp.max(parts, axis=0)
    return top + jnp.log(jnp.sum(jnp.exp(parts - top[None]), axis=0))


def lane_to_sublane(row):
    return jnp.transpose(jnp.broadcast_to(row, (LANES, LANES)))


def fold(x):
    return jnp.sum(x.reshape(x.shape[0] // 8, 8, x.shape[1]), axis=0)


def lane_group(g):
    return slice(g * LANES, (g + 1) * LANES)


def row_tile(t):
    return pl.ds(pl.multiple_of(t * LANES, LANES), LANES)


def put_copies(out_ref, value):
    for k in range(out_ref.shape[0]):
        out_ref[k] = value


def lane_tile(g):
    return pl.ds(pl.multiple_of(g * LANES, LANES), LANES)


def logit_block(k_ref, ok, t, g):
    block = k_ref[row_tile(t), lane_tile(g)]
    return jnp.where(ok, jnp.log(block), block)


def within(peak, *pots):
    for pot in pots:
        pot = jnp.abs(pot)
        for k in range(pot.shape[0] // 8):
            peak = jnp.maximum(peak, pot[8 * k : 8 * k + 8, :])
    return jnp.max(peak) <= LIM


def row_lse_exact(k_ref, ok, pot_ref, out_ref):
    tiles, groups = k_ref.shape[0] // LANES, k_ref.shape[1] // LANES

    def group(g, carry):
        def shifted(t):
            z = logit_block(k_ref, ok, t, g)
            return z if pot_ref is None else z + lane_to_sublane(pot_ref[pl.ds(t, 1), :])

        def top_of(t, top):
            return jnp.maximum(top, jnp.max(shifted(t), axis=0, keepdims=True))

        top = lax.fori_loop(0, tiles, top_of, jnp.full((1, LANES), -3.0e38, F32))

        def sum_of(t, total):
            return total + jnp.sum(jnp.exp(shifted(t) - top), axis=0, keepdims=True)

        total = lax.fori_loop(0, tiles, sum_of, jnp.zeros((1, LANES), F32))
        out_ref[pl.ds(g, 1), :] = top + jnp.log(total)
        return carry

    lax.fori_loop(0, groups, group, 0)


def col_lse_exact(k_ref, ok, pot_ref, out_ref):
    tiles, groups = k_ref.shape[0] // LANES, k_ref.shape[1] // LANES

    def tile(t, carry):
        def shifted(g):
            return logit_block(k_ref, ok, t, g) + pot_ref[pl.ds(g, 1), :]

        def top_of(g, top):
            return jnp.maximum(top, shifted(g))

        top = lax.fori_loop(0, groups, top_of, jnp.full((LANES, LANES), -3.0e38, F32))
        top = jnp.broadcast_to(jnp.max(top, axis=1, keepdims=True), (LANES, LANES))

        def sum_of(g, total):
            return total + jnp.exp(shifted(g) - top)

        total = lax.fori_loop(0, groups, sum_of, jnp.zeros((LANES, LANES), F32))
        total = jnp.sum(jnp.transpose(total), axis=0, keepdims=True)
        out_ref[pl.ds(t, 1), :] = jnp.transpose(top)[0:1, :] + jnp.log(total)
        return carry

    lax.fori_loop(0, tiles, tile, 0)


def logits_kernel(cent_hbm, vec_hbm, k_ref, peak_ref, out_ref, lse_ref, cent_ref, vec_ref, sems):
    cents, rows = k_ref.shape
    groups = rows // LANES
    step, chunk = cents // CHUNKS, rows // CHUNKS

    def pieces(hbm_ref, vmem_ref, first, size):
        return [
            pltpu.make_async_copy(
                hbm_ref.at[pl.ds(c * size, size), :], vmem_ref.at[pl.ds(c * size, size), :], sems.at[first + c]
            )
            for c in range(CHUNKS)
        ]

    vec_copies = pieces(vec_hbm, vec_ref, 0, chunk)
    cent_copies = pieces(cent_hbm, cent_ref, CHUNKS, step)
    for copy in vec_copies[:1] + cent_copies + vec_copies[1:]:
        copy.start()

    def dots(c):
        vec_copies[c].wait()
        if c == 0:
            for copy in cent_copies:
                copy.wait()
        return lax.dot_general(
            cent_ref[...], vec_ref[c * chunk : (c + 1) * chunk, :],
            (((1,), (1,)), ((), ())), preferred_element_type=F32,
        )

    peak = jnp.zeros((8, LANES), F32)
    ahead = dots(0)
    for c in range(CHUNKS):
        block = ahead
        if c + 1 < CHUNKS:
            ahead = dots(c + 1)
        for g in range(chunk // LANES):
            group = c * (chunk // LANES) + g
            total = jnp.zeros((8, LANES), F32)
            for t in range(cents // LANES):
                part = block[t * LANES : (t + 1) * LANES, lane_group(g)]
                peak = jnp.maximum(peak, jnp.max(jnp.abs(part).reshape(LANES // 8, 8, LANES), axis=0))
                part = jnp.exp2(part * (4.0 * LOG2E))
                k_ref[t * LANES : (t + 1) * LANES, lane_group(group)] = part
                total = total + fold(part)
            lse_ref[group : group + 1, :] = jnp.sum(total, axis=0, keepdims=True)
    peak = 4.0 * peak
    lse_ref[...] = jnp.log(lse_ref[...])
    peak_ref[...] = peak

    @pl.when(jnp.logical_not(within(peak)))
    def _():
        def tile(t, carry):
            def group(g, carry):
                k_ref[row_tile(t), lane_tile(g)] = 4.0 * lax.dot_general(
                    cent_ref[row_tile(t), :], vec_ref[row_tile(g), :],
                    (((1,), (1,)), ((), ())), preferred_element_type=F32,
                )
                return carry

            return lax.fori_loop(0, groups, group, carry)

        lax.fori_loop(0, cents // LANES, tile, 0)
        row_lse_exact(k_ref, False, None, lse_ref)

    put_copies(out_ref, lse_ref[...])


def row_kernel(log_target, got_ref, peak_ref, k_ref, out_ref, pot_ref, lse_ref):
    tiles, groups = k_ref.shape[0] // LANES, k_ref.shape[1] // LANES
    pot = log_target - combine_lse(got_ref[...])
    fast = within(peak_ref[...], pot)

    scales = jnp.exp(pot)
    sums = [jnp.zeros((8, LANES), F32)] * groups
    for t in range(tiles):
        scale = lane_to_sublane(scales[t : t + 1, :])
        for g in range(groups):
            sums[g] = sums[g] + fold(k_ref[t * LANES : (t + 1) * LANES, lane_group(g)] * scale)
    for g in range(groups):
        lse_ref[g : g + 1, :] = jnp.sum(sums[g], axis=0, keepdims=True)
    lse_ref[...] = jnp.log(lse_ref[...])

    @pl.when(jnp.logical_not(fast))
    def _():
        pot_ref[...] = pot
        row_lse_exact(k_ref, within(peak_ref[...]), pot_ref, lse_ref)

    put_copies(out_ref, lse_ref[...])


def col_kernel(got_ref, peak_ref, k_ref, out_ref, lse_ref, pot_ref):
    tiles, groups = k_ref.shape[0] // LANES, k_ref.shape[1] // LANES
    pot = -combine_lse(got_ref[...])
    fast = within(peak_ref[...], pot)

    scale = jnp.exp(pot)
    for t in range(tiles):
        total = jnp.zeros((LANES, LANES), F32)
        for g in range(groups):
            total = total + k_ref[t * LANES : (t + 1) * LANES, lane_group(g)] * scale[g : g + 1, :]
        lse_ref[t : t + 1, :] = jnp.sum(jnp.transpose(total), axis=0, keepdims=True)
    lse_ref[...] = jnp.log(lse_ref[...])

    @pl.when(jnp.logical_not(fast))
    def _():
        pot_ref[...] = pot
        col_lse_exact(k_ref, within(peak_ref[...]), pot_ref, lse_ref)

    put_copies(out_ref, lse_ref[...])


def sums_kernel(log_target, flips, *refs):
    first_call = log_target is not None
    cols_ref, rows_ref, peak_ref, k_ref, vec_ref, a_ref, b_ref = refs[:7]
    plan_ref, col_ref, row_ref = refs[-3:]
    groups = k_ref.shape[1] // LANES
    if first_call:
        col_pot = log_target - combine_lse(cols_ref[...])
        row_pot = -combine_lse(rows_ref[...])
        for pot_ref in refs[7:9]:
            pot_ref[...] = col_pot
        for pot_ref in refs[9:11]:
            pot_ref[...] = row_pot
    else:
        col_pot, row_pot = cols_ref[...], rows_ref[...]
    fast = within(peak_ref[...], col_pot, row_pot)
    col_ref[...] = jnp.exp(col_pot)
    row_scale = jnp.exp(row_pot)
    bits = position_bits()
    x1, z1 = bits[XB1], bits[ZB1]
    tiles = []
    for chain, (first, second) in enumerate(((x1, z1), (z1, x1))):
        first = 1 - first if flips[0] else first
        second = 1 - second if flips[1] else second
        tiles.append(chain * 4 + first * 2 + second)

    def put_mass(total, out_ref):
        mass = jnp.broadcast_to(jnp.sum(total, axis=1, keepdims=True), (LANES, LANES))
        lane = lax.broadcasted_iota(jnp.int32, (8, LANES), 1) // (LANES // PARTS)
        for b in range(LANES // BLOCK):
            unit = mass[b * BLOCK : b * BLOCK + 8, :]
            for k in range(1, PARTS):
                at = b * BLOCK + 8 * k
                unit = jnp.where(lane == k, mass[at : at + 8, :], unit)
            out_ref[b, out_ref.shape[1] - 1] = unit

    for chain, (tile, out_ref) in enumerate(zip(tiles, (a_ref, b_ref))):
        scale = lane_to_sublane(col_ref[pl.ds(tile, 1), :])
        total = jnp.zeros((LANES, LANES), F32)
        for g in range(groups):
            plan = k_ref[row_tile(tile), lane_group(g)] * row_scale[g : g + 1, :] * scale
            total = total + plan
            plan_ref[chain * LANES : (chain + 1) * LANES, lane_group(g)] = plan.astype(jnp.bfloat16)
        put_mass(total, out_ref)

    @pl.when(jnp.logical_not(fast))
    def _():
        ok = within(peak_ref[...])
        col_ref[...] = col_pot
        row_ref[...] = row_pot
        for chain, (tile, out_ref) in enumerate(zip(tiles, (a_ref, b_ref))):
            shift = lane_to_sublane(col_ref[pl.ds(tile, 1), :])

            def group(g, total):
                plan = jnp.exp(logit_block(k_ref, ok, tile, g) + row_ref[pl.ds(g, 1), :] + shift)
                plan_ref[chain * LANES : (chain + 1) * LANES, lane_tile(g)] = plan.astype(jnp.bfloat16)
                return total + plan

            put_mass(lax.fori_loop(0, groups, group, jnp.zeros((LANES, LANES), F32)), out_ref)

    block = jnp.dot(plan_ref[...], vec_ref[...], preferred_element_type=F32)
    across = block.shape[1] // LANES
    for chain, out_ref in enumerate((a_ref, b_ref)):
        for b in range(LANES // BLOCK):
            for k in range(PARTS):
                row = chain * LANES + b * BLOCK + 8 * k
                for g in range(across):
                    out_ref[b, k * across + g] = block[row : row + 8, lane_group(g)]


def add_kernel(mine_ref, got_ref, out_ref):
    out_ref[...] = mine_ref[...] + got_ref[...]


def spot(flips):
    bits = position_bits()
    x2, z2 = bits[XB2], bits[ZB2]
    return (1 - x2 if flips[0] else x2) * 2 + (1 - z2 if flips[1] else z2)


def pieces_kernel(order, mine_ref, first_ref, second_ref, send_ref, keep_ref):
    for n, flips in enumerate(order):
        at = spot(flips)
        out_ref = (send_ref, keep_ref)[n // 2]
        out_ref[n % 2] = mine_ref[at] + first_ref[at] + second_ref[at]


def own_kernel(keep_ref, got_ref, second_ref, out_ref):
    out_ref[...] = keep_ref[1] + got_ref[1] + second_ref[...]


def hold_kernel(keep_ref, got_ref, out_ref):
    out_ref[...] = keep_ref[0] + got_ref[0]


def mean_kernel(sum_ref, got_ref, out_ref):
    units = sum_ref.shape[0] - 1
    across = out_ref.shape[1] // LANES
    lanes = LANES // PARTS
    mass = sum_ref[units] + got_ref[units]
    for k in range(PARTS):
        part = jnp.broadcast_to(mass[:, k * lanes : k * lanes + 1], (8, LANES))
        for g in range(across):
            u = k * across + g
            out_ref[8 * k : 8 * k + 8, lane_group(g)] = (sum_ref[u] + got_ref[u]) / part


def join_kernel(order, *refs):
    out_ref = refs[-1]
    for flips, part_ref in zip(order, refs):
        at = pl.ds(pl.multiple_of(spot(flips) * BLOCK, BLOCK), BLOCK)
        out_ref[at, :] = part_ref[...]


def place_kernel(spots, *refs):
    out_ref, sems = refs[-2:]
    bits = position_bits()
    x1, z1 = bits[XB1], bits[ZB1]
    copies = []
    for n, ((chain, flips), part_ref) in enumerate(zip(spots, refs)):
        size = part_ref.shape[0]
        first, second = (z1, x1) if chain else (x1, z1)
        first = 1 - first if flips[0] else first
        second = 1 - second if flips[1] else second
        at = pl.ds(pl.multiple_of((chain * 4 + first * 2 + second) * size, size), size)
        copies.append(pltpu.make_async_copy(part_ref, out_ref.at[at, :], sems.at[n]))
    for copy in copies:
        copy.start()
    for copy in copies:
        copy.wait()


def place(row, core):
    return (row // ZS + (XS - 1) * core) % XS, (row % ZS + (ZS - 1) * core) % ZS


def pairs(partner, n_cols):
    out = []
    for row in range(XS * ZS):
        for col in range(n_cols):
            core = col % 2
            x, z = partner(*place(row, core))
            to = (x + core) % XS * ZS + (z + core) % ZS
            out.append((row * n_cols + col, to * n_cols + col))
    return out


def exchange(x, partner):
    return lax.ppermute(x, ("rows", "cols"), pairs(partner, lax.axis_size("cols")))


def x_first(x, z):
    return x ^ 1, z


def x_second(x, z):
    return XS - 1 - x, z


def z_first(x, z):
    return x, z ^ 1


def z_second(x, z):
    return x, (z - 1 + 2 * (z % 2)) % ZS


def z_third(x, z):
    return x, {0: 3, 3: 0, 1: 6, 6: 1, 2: 5, 5: 2, 4: 7, 7: 4}[z]


def position_bits():
    core = lax.axis_index("cols") & 1
    row = lax.axis_index("rows")
    x = ((row >> 3) + (XS - 1) * core) & (XS - 1)
    z = (row + (ZS - 1) * core) & (ZS - 1)
    return (x ^ (x >> 1)) & 1, x >> 1, ((z + 1) >> 1) & 1, (0xB4 >> z) & 1


def add(mine, got):
    return pl.pallas_call(
        add_kernel,
        out_shape=jax.ShapeDtypeStruct(mine.shape, F32),
        in_specs=[vmem(), vmem()],
        out_specs=vmem(),
        compiler_params=params(4),
        name="add",
    )(mine, got)


def put(spots, parts, cents, *before):
    return pl.pallas_call(
        functools.partial(place_kernel, spots),
        out_shape=jax.ShapeDtypeStruct((cents, parts[0].shape[1]), F32),
        in_specs=[vmem()] * len(parts) + [hbm()] * len(before),
        out_specs=hbm(),
        scratch_shapes=[pltpu.SemaphoreType.DMA((len(parts),))],
        input_output_aliases={len(parts): 0} if before else {},
        compiler_params=params(4),
        name="place",
    )(*parts, *before)


A_ORDER = ((True, True), (True, False), (False, True), (False, False))
B_ORDER = ((True, True), (False, True), (True, False), (False, False))


def sum_of_four(order, first, second, *terms):
    piece = jax.ShapeDtypeStruct(terms[0].shape[1:], F32)
    pair = jax.ShapeDtypeStruct((2, *terms[0].shape[1:]), F32)
    send, keep = pl.pallas_call(
        functools.partial(pieces_kernel, order),
        out_shape=(pair, pair),
        in_specs=[vmem()] * 3,
        out_specs=(vmem(), vmem()),
        compiler_params=params(4),
        name="pieces",
    )(*terms)
    got = exchange(send, first)
    hold = pl.pallas_call(
        hold_kernel,
        out_shape=piece,
        in_specs=[vmem()] * 2,
        out_specs=vmem(),
        compiler_params=params(4),
        name="hold",
    )(keep, got)
    return pl.pallas_call(
        own_kernel,
        out_shape=piece,
        in_specs=[vmem()] * 3,
        out_specs=vmem(),
        compiler_params=params(4),
        name="own",
    )(keep, got, exchange(hold, second))


def mean_of_four(order, first, second, mine, got, width):
    mean = pl.pallas_call(
        mean_kernel,
        out_shape=jax.ShapeDtypeStruct((BLOCK, width), F32),
        in_specs=[vmem()] * 2,
        out_specs=vmem(),
        compiler_params=params(4),
        name="mean",
    )(mine, got)
    hold, stay = exchange(mean, second), exchange(mean, first)
    away = exchange(hold, first)
    return pl.pallas_call(
        functools.partial(join_kernel, order),
        out_shape=jax.ShapeDtypeStruct((4 * BLOCK, width), F32),
        in_specs=[vmem()] * 4,
        out_specs=vmem(),
        compiler_params=params(4),
        name="join",
    )(away, stay, hold, mean)


def mean_over_rows(quarter_sums, cents, width):
    pass_a, pass_b = quarter_sums((True, True))
    pass_a, pass_b = exchange(pass_a, x_first), exchange(pass_b, z_first)
    stay_a, stay_b = quarter_sums((True, False))
    stay_a, stay_b = exchange(stay_a, x_first), exchange(stay_b, z_first)
    mine_a, mine_b = quarter_sums((False, True))
    next_a = exchange(add(mine_a, pass_a), z_first)
    next_b = exchange(add(mine_b, pass_b), x_first)
    mine_a, mine_b = quarter_sums((False, False))
    mine_a = sum_of_four(A_ORDER, x_second, z_second, mine_a, stay_a, next_a)
    mine_b = sum_of_four(B_ORDER, z_second, x_second, mine_b, stay_b, next_b)
    got_a, got_b = exchange(mine_a, z_third), exchange(mine_b, z_third)
    mine_a = mean_of_four(A_ORDER, x_second, z_second, mine_a, got_a, width)
    mine_b = mean_of_four(B_ORDER, z_second, x_second, mine_b, got_b, width)
    next_a, next_b = exchange(mine_a, z_first), exchange(mine_b, x_first)
    stay_a, stay_b = exchange(mine_a, x_first), exchange(mine_b, z_first)
    pass_a, pass_b = exchange(next_a, x_first), exchange(next_b, z_first)
    near = ((0, (False, False)), (1, (False, False)), (0, (False, True)), (1, (False, True)))
    out = put(near, (mine_a, mine_b, next_a, next_b), cents)
    out = put(((0, (True, False)), (1, (True, False))), (stay_a, stay_b), cents, out)
    return put(((0, (True, True)), (1, (True, True))), (pass_a, pass_b), cents, out)


def vmem():
    return pl.BlockSpec(memory_space=pltpu.VMEM)


def hbm():
    return pl.BlockSpec(memory_space=pltpu.HBM)


def pinned(x):
    return pltpu.with_memory_space_constraint(x, pltpu.VMEM)


def params(mib):
    return pltpu.CompilerParams(vmem_limit_bytes=mib * MIB)


def per_device(vectors, centroids):
    n_rows, n_cols = lax.axis_size("rows"), lax.axis_size("cols")
    rows, width = vectors.shape
    cents = centroids.shape[0]
    log_target = math.log(rows * n_rows / (cents * n_cols))
    groups, tiles = rows // LANES, cents // LANES
    kept = pltpu.VMEM((cents, rows), F32)
    peak_type = jax.ShapeDtypeStruct((8, LANES), F32)
    row_parts = jax.ShapeDtypeStruct((n_cols, groups, LANES), F32)
    col_parts = jax.ShapeDtypeStruct((n_rows, tiles, LANES), F32)
    row_scratch = pltpu.VMEM((groups, LANES), F32)
    col_scratch = pltpu.VMEM((tiles, LANES), F32)

    kernel, peak, part = pl.pallas_call(
        logits_kernel,
        out_shape=(kept, peak_type, row_parts),
        in_specs=[hbm(), hbm()],
        out_specs=(vmem(), vmem(), vmem()),
        scratch_shapes=[
            row_scratch,
            pltpu.VMEM((cents, width), jnp.bfloat16),
            pltpu.VMEM((rows, width), jnp.bfloat16),
            pltpu.SemaphoreType.DMA((2 * CHUNKS,)),
        ],
        compiler_params=params(24),
        name="logits",
    )(*(pltpu.with_memory_space_constraint(x, pltpu.HBM) for x in (centroids, vectors)))

    for step in range(ITERS):
        row_got = lax.all_to_all(part, "cols", 0, 0, tiled=True)
        part = pl.pallas_call(
            col_kernel,
            out_shape=col_parts,
            in_specs=[vmem(), vmem(), vmem()],
            out_specs=vmem(),
            scratch_shapes=[col_scratch, row_scratch],
            compiler_params=params(4),
            name="col_step",
        )(row_got, peak, pinned(kernel))
        col_got = lax.all_to_all(part, "rows", 0, 0, tiled=True)
        part = pl.pallas_call(
            functools.partial(row_kernel, log_target),
            out_shape=row_parts,
            in_specs=[vmem(), vmem(), vmem()],
            out_specs=vmem(),
            scratch_shapes=[col_scratch, row_scratch],
            compiler_params=params(4),
            name="row_step",
        )(col_got, peak, pinned(kernel))
    row_got = lax.all_to_all(part, "cols", 0, 0, tiled=True)

    quarter = jax.ShapeDtypeStruct((LANES // BLOCK, PARTS * (width // LANES) + 1, 8, LANES), F32)
    pots = []

    def quarter_sums(flips):
        first = not pots
        pot_types = tuple(jax.ShapeDtypeStruct((n, LANES), F32) for n in (tiles, tiles, groups, groups))
        a, b, *new = pl.pallas_call(
            functools.partial(sums_kernel, log_target if first else None, flips),
            out_shape=(quarter, quarter) + (pot_types if first else ()),
            in_specs=[vmem()] * 5,
            out_specs=(vmem(),) * (6 if first else 2),
            scratch_shapes=[pltpu.VMEM((2 * LANES, rows), jnp.bfloat16), col_scratch, row_scratch],
            compiler_params=params(8),
            cost_estimate=pl.CostEstimate(
                flops=rows * cents * width // 2, bytes_accessed=4 * MIB, transcendentals=0
            ),
            name="sums",
        )(*(pots[1::2] or (col_got, row_got)), peak, pinned(kernel), vectors)
        pots.extend(new)
        return a, b

    new_centroids = mean_over_rows(quarter_sums, cents, width)
    col_pot, row_pot = pots[0::2]
    return (new_centroids, row_pot.reshape(rows), col_pot.reshape(cents))


def solution(mesh):
    return jax.shard_map(
        per_device,
        mesh=mesh,
        in_specs=(P("rows", None), P("cols", None)),
        out_specs=(P("cols", None), P("rows"), P("cols")),
        check_vma=False,
    )
```

profile of v0, /device:TPU:8, one launch (start us, length us, event | category | flops | bytes accessed | tf_op | source)
XLA Modules:
  0.0 320.0 jit_solution(453115277426789989)
XLA Ops:
  0.6 40.4 %logits.1 = (f32[1024,2048]{1,0:T(8,128)S(1)}, f32[8,128]{1,0:T(8,128)S(1)}, f32[8,16,128]{2,1,0:T(8,128)S(1)}) custom-call(bf16[1024,768]{1,0:T(8,128)(2,1)} %cent_hbm.1, bf16[2048,768]{1,0:T(8,128)(2,1)} %refs_4_.7), custom_call_target="tpu_custom_call" | custom-call | tf_op jit(solution)/shard_map/logits/pallas_call | solution.py:533
  41.0 8.9 %all_to_all.35.got_ref = f32[8,16,128]{2,1,0:T(8,128)S(1)} all-to-all(f32[8,16,128]{2,1,0:T(8,128)S(1)} %get-tuple-element.22), channel_id=1, replica_groups=mesh['rows'=32,'cols'=8] {'cols'}, dimensions={0} | all-to-all | bytes 131072 | tf_op jit(solution)/shard_map/all_to_all | solution.py:549
  49.9 9.4 %col_step.3 = f32[32,8,128]{2,1,0:T(8,128)S(1)} custom-call(f32[8,16,128]{2,1,0:T(8,128)S(1)} %all_to_all.35.got_ref, f32[8,128]{1,0:T(8,128)S(1)} %get-tuple-element.23.peak_ref.refs_2_, f32[1024,2048]{1,0:T(8,128)S(1)} %get-tuple-element.24.k_ref.refs_3_), custom_call_target="tpu_custom_call" | custom-call | tf_op jit(solution)/shard_map/col_step/pallas_call | solution.py:550
  59.3 21.4 %all_to_all.36.got_ref = f32[32,8,128]{2,1,0:T(8,128)S(1)} all-to-all(f32[32,8,128]{2,1,0:T(8,128)S(1)} %col_step.3), channel_id=1, replica_groups=mesh['rows'=32,'cols'=8] {'rows'}, dimensions={0} | all-to-all | bytes 262144 | tf_op jit(solution)/shard_map/all_to_all | solution.py:559
  80.6 30.3 %row_step.3 = f32[8,16,128]{2,1,0:T(8,128)S(1)} custom-call(f32[32,8,128]{2,1,0:T(8,128)S(1)} %all_to_all.36.got_ref, f32[8,128]{1,0:T(8,128)S(1)} %get-tuple-element.23.peak_ref.refs_2_, f32[1024,2048]{1,0:T(8,128)S(1)} %get-tuple-element.24.k_ref.refs_3_), custom_call_target="tpu_custom_call" | custom-call | tf_op jit(solution)/shard_map/row_step/pallas_call | solution.py:560
  111.0 8.0 %all_to_all.37.got_ref = f32[8,16,128]{2,1,0:T(8,128)S(1)} all-to-all(f32[8,16,128]{2,1,0:T(8,128)S(1)} %row_step.3), channel_id=1, replica_groups=mesh['rows'=32,'cols'=8] {'cols'}, dimensions={0} | all-to-all | bytes 131072 | tf_op jit(solution)/shard_map/all_to_all | solution.py:549
  119.0 9.4 %col_step.4 = f32[32,8,128]{2,1,0:T(8,128)S(1)} custom-call(f32[8,16,128]{2,1,0:T(8,128)S(1)} %all_to_all.37.got_ref, f32[8,128]{1,0:T(8,128)S(1)} %get-tuple-element.23.peak_ref.refs_2_, f32[1024,2048]{1,0:T(8,128)S(1)} %get-tuple-element.24.k_ref.refs_3_), custom_call_target="tpu_custom_call" | custom-call | tf_op jit(solution)/shard_map/col_step/pallas_call | solution.py:550
  128.4 13.9 %all_to_all.38.got_ref = f32[32,8,128]{2,1,0:T(8,128)S(1)} all-to-all(f32[32,8,128]{2,1,0:T(8,128)S(1)} %col_step.4), channel_id=1, replica_groups=mesh['rows'=32,'cols'=8] {'rows'}, dimensions={0} | all-to-all | bytes 262144 | tf_op jit(solution)/shard_map/all_to_all | solution.py:559
  142.2 30.3 %row_step.4 = f32[8,16,128]{2,1,0:T(8,128)S(1)} custom-call(f32[32,8,128]{2,1,0:T(8,128)S(1)} %all_to_all.38.got_ref, f32[8,128]{1,0:T(8,128)S(1)} %get-tuple-element.23.peak_ref.refs_2_, f32[1024,2048]{1,0:T(8,128)S(1)} %get-tuple-element.24.k_ref.refs_3_), custom_call_target="tpu_custom_call" | custom-call | tf_op jit(solution)/shard_map/row_step/pallas_call | solution.py:560
  172.6 8.0 %all_to_all.39.got_ref = f32[8,16,128]{2,1,0:T(8,128)S(1)} all-to-all(f32[8,16,128]{2,1,0:T(8,128)S(1)} %row_step.4), channel_id=1, replica_groups=mesh['rows'=32,'cols'=8] {'cols'}, dimensions={0} | all-to-all | bytes 131072 | tf_op jit(solution)/shard_map/all_to_all | solution.py:549
  180.6 9.4 %col_step.5 = f32[32,8,128]{2,1,0:T(8,128)S(1)} custom-call(f32[8,16,128]{2,1,0:T(8,128)S(1)} %all_to_all.39.got_ref, f32[8,128]{1,0:T(8,128)S(1)} %get-tuple-element.23.peak_ref.refs_2_, f32[1024,2048]{1,0:T(8,128)S(1)} %get-tuple-element.24.k_ref.refs_3_), custom_call_target="tpu_custom_call" | custom-call | tf_op jit(solution)/shard_map/col_step/pallas_call | solution.py:550
  190.0 13.9 %all_to_all.40.got_ref.refs_0_ = f32[32,8,128]{2,1,0:T(8,128)S(1)} all-to-all(f32[32,8,128]{2,1,0:T(8,128)S(1)} %col_step.5), channel_id=1, replica_groups=mesh['rows'=32,'cols'=8] {'rows'}, dimensions={0} | all-to-all | bytes 262144 | tf_op jit(solution)/shard_map/all_to_all | solution.py:559
  203.8 30.3 %row_step.5 = f32[8,16,128]{2,1,0:T(8,128)S(1)} custom-call(f32[32,8,128]{2,1,0:T(8,128)S(1)} %all_to_all.40.got_ref.refs_0_, f32[8,128]{1,0:T(8,128)S(1)} %get-tuple-element.23.peak_ref.refs_2_, f32[1024,2048]{1,0:T(8,128)S(1)} %get-tuple-element.24.k_ref.refs_3_), custom_call_target="tpu_custom_call" | custom-call | tf_op jit(solution)/shard_map/row_step/pallas_call | solution.py:560
  234.1 8.0 %all_to_all.41.refs_1_ = f32[8,16,128]{2,1,0:T(8,128)S(1)} all-to-all(f32[8,16,128]{2,1,0:T(8,128)S(1)} %row_step.5), channel_id=1, replica_groups=mesh['rows'=32,'cols'=8] {'cols'}, dimensions={0} | all-to-all | bytes 131072 | tf_op jit(solution)/shard_map/all_to_all | solution.py:569
  242.1 3.3 %sums.4 = (f32[4,25,8,128]{3,2,1,0:T(8,128)S(1)}, f32[4,25,8,128]{3,2,1,0:T(8,128)S(1)}, f32[8,128]{1,0:T(8,128)}, f32[8,128]{1,0:T(8,128)S(1)}, f32[16,128]{1,0:T(8,128)}, /*index=5*/f32[16,128]{1,0:T(8,128)S(1)}) custom-call(f32[32,8,128]{2,1,0:T(8,128)S(1)} %all_to_all.40.got_ref.refs_0_, f32[8,16,128]{2,1,0:T(8,128)S(1)} %all_to_all.41.refs_1_, ...), custom_call_target="tpu_custom_call" | custom-call | flops 805306368 | bytes 4194304 | tf_op jit(solution)/shard_map/sums/pallas_call | solution.py:577
  245.4 0.6 collective-permute-start.1
  246.1 1.3 collective-permute-start.12
  247.3 2.9 sums.6
  250.2 1.5 collective-permute-start
  251.7 2.9 sums.7
  254.5 0.0 collective-permute-done.1.got_ref
  254.6 0.9 collective-permute-start.2
  255.5 1.3 collective-permute-start.11
  256.7 0.0 collective-permute-done.12.got_ref
  256.8 0.7 collective-permute-start.13
  257.5 2.9 sums.5
  260.4 2.3 collective-permute-done.2.second_ref
  262.6 0.1 pieces.2
  262.7 1.3 collective-permute-start.3
  264.0 3.1 collective-permute-done.11.first_ref
  267.0 0.1 pieces.3
  267.1 0.7 collective-permute-start.14
  267.8 2.0 collective-permute-done.3.got_ref
  269.8 0.8 collective-permute-start.4
  270.5 3.6 %collective-permute-done.14.got_ref = f32[2,25,8,128]{3,2,1,0:T(8,128)S(1)} collective-permute-done((f32[2,25,8,128]{3,2,1,0:T(8,128)S(1)}, f32[2,25,8,128]{3,2,1,0:T(8,128)S(1)}, u32[]{:S(2)}, u32[]{:S(2)}) %collective-permute-start.14) | collective-permute-done | bytes 204832 | tf_op jit(solution)/shard_map/ppermute | solution.py:371
  274.2 1.3 collective-permute-start.15
  275.4 0.3 collective-permute-done.4.second_ref
  275.8 1.6 collective-permute-start.5
  277.4 2.7 collective-permute-done.15.second_ref
  280.2 1.6 collective-permute-start.16
  281.8 3.6 %collective-permute-done.5.got_ref = f32[25,8,128]{2,1,0:T(8,128)S(1)} collective-permute-done((f32[25,8,128]{2,1,0:T(8,128)S(1)}, f32[25,8,128]{2,1,0:T(8,128)S(1)}, u32[]{:S(2)}, u32[]{:S(2)}) %collective-permute-start.5) | collective-permute-done | bytes 102432 | tf_op jit(solution)/shard_map/ppermute | solution.py:371
  285.4 0.1 mean.2.refs_3_
  285.5 0.1 collective-permute-start.6
  285.6 1.8 collective-permute-done.16.got_ref
  287.4 0.1 mean.3.refs_3_
  287.4 2.0 collective-permute-start.17
  289.5 1.3 collective-permute-start.8
  290.8 0.6 collective-permute-done.6.refs_2_
  291.4 2.3 collective-permute-start.7
  293.7 0.8 collective-permute-start.19
  294.5 2.4 collective-permute-start.18
  297.0 1.3 collective-permute-done.7.refs_0_
  298.3 1.1 collective-permute-start.9
  299.4 1.0 collective-permute-done.19.refs_1_
  300.5 2.1 collective-permute-done.18.refs_0_
  302.6 0.1 collective-permute-start.20
  302.7 2.0 collective-permute-start.22
  304.7 1.5 collective-permute-done.9.refs_2_
  306.2 4.3 %collective-permute-done.20.refs_3_ = f32[128,768]{1,0:T(8,128)S(1)} collective-permute-done((f32[128,768]{1,0:T(8,128)S(1)}, f32[128,768]{1,0:T(8,128)S(1)}, u32[]{:S(2)}, u32[]{:S(2)}) %collective-permute-start.20) | collective-permute-done | bytes 393248 | tf_op jit(solution)/shard_map/ppermute | solution.py:371
  310.5 1.2 place.3.refs_2_
  311.7 3.0 collective-permute-done.22.refs_0_
  314.7 0.9 place.4.refs_2_
  315.6 3.3 %collective-permute-done.10.refs_0_ = f32[128,768]{1,0:T(8,128)S(1)} collective-permute-done((f32[128,768]{1,0:T(8,128)S(1)}, f32[128,768]{1,0:T(8,128)S(1)}, u32[]{:S(2)}, u32[]{:S(2)}) %collective-permute-start.10) | collective-permute-done | bytes 393248 | tf_op jit(solution)/shard_map/ppermute | solution.py:371
  318.9 0.9 place.5
  (19 shorter events, 0.3 us)
Async XLA Ops:
  203.8 38.3 %copy-start = (bf16[2048,768]{1,0:T(8,128)(2,1)S(1)}, bf16[2048,768]{1,0:T(8,128)(2,1)}, u32[]{:S(2)}) copy-start(bf16[2048,768]{1,0:T(8,128)(2,1)} %refs_4_.7) | copy-start | bytes 9437188
  245.4 9.1 %collective-permute-start.1 = (f32[4,25,8,128]{3,2,1,0:T(8,128)S(1)}, f32[4,25,8,128]{3,2,1,0:T(8,128)S(1)}, u32[]{:S(2)}, u32[]{:S(2)}) collective-permute-start(f32[4,25,8,128]{3,2,1,0:T(8,128)S(1)} %get-tuple-element.30), channel_id=1, source_target_pairs={{0,64},{1,193},{2,66},{3,195},{4,68},{5,197},{6,70},{7,199},{8,72}... | collective-permute-start | bytes 1228808 | tf_op jit(solution)/shard_map/ppermute | solution.py:371
  246.1 10.7 %collective-permute-start.12 = (f32[4,25,8,128]{3,2,1,0:T(8,128)S(1)}, f32[4,25,8,128]{3,2,1,0:T(8,128)S(1)}, u32[]{:S(2)}, u32[]{:S(2)}) collective-permute-start(f32[4,25,8,128]{3,2,1,0:T(8,128)S(1)} %get-tuple-element.36), channel_id=1, source_target_pairs={{0,8},{1,57},{2,10},{3,59},{4,12},{5,61},{6,14},{7,63},{8,0},{9,17... | collective-permute-start | bytes 1228808 | tf_op jit(solution)/shard_map/ppermute | solution.py:371
  250.2 10.2 %collective-permute-start = (f32[4,25,8,128]{3,2,1,0:T(8,128)S(1)}, f32[4,25,8,128]{3,2,1,0:T(8,128)S(1)}, u32[]{:S(2)}, u32[]{:S(2)}) collective-permute-start(f32[4,25,8,128]{3,2,1,0:T(8,128)S(1)} %get-tuple-element.28), channel_id=1, source_target_pairs={{0,64},{1,193},{2,66},{3,195},{4,68},{5,197},{6,70},{7,199},{8,72}... | collective-permute-start | bytes 1228808 | tf_op jit(solution)/shard_map/ppermute | solution.py:371
  254.6 8.0 %collective-permute-start.2 = (f32[4,25,8,128]{3,2,1,0:T(8,128)S(1)}, f32[4,25,8,128]{3,2,1,0:T(8,128)S(1)}, u32[]{:S(2)}, u32[]{:S(2)}) collective-permute-start(f32[4,25,8,128]{3,2,1,0:T(8,128)S(1)} %add.2), channel_id=1, source_target_pairs={{0,8},{1,57},{2,10},{3,59},{4,12},{5,61},{6,14},{7,63},{8,0},{9,17... | collective-permute-start | bytes 1228808 | tf_op jit(solution)/shard_map/ppermute | solution.py:371
  255.5 11.6 %collective-permute-start.11 = (f32[4,25,8,128]{3,2,1,0:T(8,128)S(1)}, f32[4,25,8,128]{3,2,1,0:T(8,128)S(1)}, u32[]{:S(2)}, u32[]{:S(2)}) collective-permute-start(f32[4,25,8,128]{3,2,1,0:T(8,128)S(1)} %get-tuple-element.34), channel_id=1, source_target_pairs={{0,8},{1,57},{2,10},{3,59},{4,12},{5,61},{6,14},{7,63},{8,0},{9,17... | collective-permute-start | bytes 1228808 | tf_op jit(solution)/shard_map/ppermute | solution.py:371
  256.8 10.3 %collective-permute-start.13 = (f32[4,25,8,128]{3,2,1,0:T(8,128)S(1)}, f32[4,25,8,128]{3,2,1,0:T(8,128)S(1)}, u32[]{:S(2)}, u32[]{:S(2)}) collective-permute-start(f32[4,25,8,128]{3,2,1,0:T(8,128)S(1)} %add.3), channel_id=1, source_target_pairs={{0,64},{1,193},{2,66},{3,195},{4,68},{5,197},{6,70},{7,199},{8,72}... | collective-permute-start | bytes 1228808 | tf_op jit(solution)/shard_map/ppermute | solution.py:371
  262.7 7.1 %collective-permute-start.3 = (f32[2,25,8,128]{3,2,1,0:T(8,128)S(1)}, f32[2,25,8,128]{3,2,1,0:T(8,128)S(1)}, u32[]{:S(2)}, u32[]{:S(2)}) collective-permute-start(f32[2,25,8,128]{3,2,1,0:T(8,128)S(1)} %get-tuple-element.32), channel_id=1, source_target_pairs={{0,192},{1,65},{2,194},{3,67},{4,196},{5,69},{6,198},{7,71},{8,200... | collective-permute-start | bytes 614408 | tf_op jit(solution)/shard_map/ppermute | solution.py:371
  267.1 7.1 %collective-permute-start.14 = (f32[2,25,8,128]{3,2,1,0:T(8,128)S(1)}, f32[2,25,8,128]{3,2,1,0:T(8,128)S(1)}, u32[]{:S(2)}, u32[]{:S(2)}) collective-permute-start(f32[2,25,8,128]{3,2,1,0:T(8,128)S(1)} %get-tuple-element.38), channel_id=1, source_target_pairs={{0,56},{1,9},{2,58},{3,11},{4,60},{5,13},{6,62},{7,15},{8,16},{9,1... | collective-permute-start | bytes 614408 | tf_op jit(solution)/shard_map/ppermute | solution.py:371
  269.8 6.0 %collective-permute-start.4 = (f32[25,8,128]{2,1,0:T(8,128)S(1)}, f32[25,8,128]{2,1,0:T(8,128)S(1)}, u32[]{:S(2)}, u32[]{:S(2)}) collective-permute-start(f32[25,8,128]{2,1,0:T(8,128)S(1)} %hold.2), channel_id=1, source_target_pairs={{0,56},{1,9},{2,58},{3,11},{4,60},{5,13},{6,62},{7,15},{8,16},{9,1... | collective-permute-start | bytes 307208 | tf_op jit(solution)/shard_map/ppermute | solution.py:371
  274.2 6.0 %collective-permute-start.15 = (f32[25,8,128]{2,1,0:T(8,128)S(1)}, f32[25,8,128]{2,1,0:T(8,128)S(1)}, u32[]{:S(2)}, u32[]{:S(2)}) collective-permute-start(f32[25,8,128]{2,1,0:T(8,128)S(1)} %hold.3), channel_id=1, source_target_pairs={{0,192},{1,65},{2,194},{3,67},{4,196},{5,69},{6,198},{7,71},{8,200... | collective-permute-start | bytes 307208 | tf_op jit(solution)/shard_map/ppermute | solution.py:371
  275.8 9.6 %collective-permute-start.5 = (f32[25,8,128]{2,1,0:T(8,128)S(1)}, f32[25,8,128]{2,1,0:T(8,128)S(1)}, u32[]{:S(2)}, u32[]{:S(2)}) collective-permute-start(f32[25,8,128]{2,1,0:T(8,128)S(1)} %own.2.sum_ref), channel_id=1, source_target_pairs={{0,24},{1,41},{2,26},{3,43},{4,28},{5,45},{6,30},{7,47},{8,48},{9,... | collective-permute-start | bytes 307208 | tf_op jit(solution)/shard_map/ppermute | solution.py:371
  280.2 7.2 %collective-permute-start.16 = (f32[25,8,128]{2,1,0:T(8,128)S(1)}, f32[25,8,128]{2,1,0:T(8,128)S(1)}, u32[]{:S(2)}, u32[]{:S(2)}) collective-permute-start(f32[25,8,128]{2,1,0:T(8,128)S(1)} %own.3.sum_ref), channel_id=1, source_target_pairs={{0,24},{1,41},{2,26},{3,43},{4,28},{5,45},{6,30},{7,47},{8,48},{9,... | collective-permute-start | bytes 307208 | tf_op jit(solution)/shard_map/ppermute | solution.py:371
  285.5 5.9 %collective-permute-start.6 = (f32[32,768]{1,0:T(8,128)S(1)}, f32[32,768]{1,0:T(8,128)S(1)}, u32[]{:S(2)}, u32[]{:S(2)}) collective-permute-start(f32[32,768]{1,0:T(8,128)S(1)} %mean.2.refs_3_), channel_id=1, source_target_pairs={{0,56},{1,9},{2,58},{3,11},{4,60},{5,13},{6,62},{7,15},{8,16},{9,1... | collective-permute-start | bytes 294920 | tf_op jit(solution)/shard_map/ppermute | solution.py:371
  287.4 7.1 %collective-permute-start.17 = (f32[32,768]{1,0:T(8,128)S(1)}, f32[32,768]{1,0:T(8,128)S(1)}, u32[]{:S(2)}, u32[]{:S(2)}) collective-permute-start(f32[32,768]{1,0:T(8,128)S(1)} %mean.3.refs_3_), channel_id=1, source_target_pairs={{0,192},{1,65},{2,194},{3,67},{4,196},{5,69},{6,198},{7,71},{8,200... | collective-permute-start | bytes 294920 | tf_op jit(solution)/shard_map/ppermute | solution.py:371
  289.5 7.5 %collective-permute-start.8 = (f32[32,768]{1,0:T(8,128)S(1)}, f32[32,768]{1,0:T(8,128)S(1)}, u32[]{:S(2)}, u32[]{:S(2)}) collective-permute-start(f32[32,768]{1,0:T(8,128)S(1)} %mean.2.refs_3_), channel_id=1, source_target_pairs={{0,192},{1,65},{2,194},{3,67},{4,196},{5,69},{6,198},{7,71},{8,200... | collective-permute-start | bytes 294920 | tf_op jit(solution)/shard_map/ppermute | solution.py:371
  291.4 6.9 %collective-permute-start.7 = (f32[32,768]{1,0:T(8,128)S(1)}, f32[32,768]{1,0:T(8,128)S(1)}, u32[]{:S(2)}, u32[]{:S(2)}) collective-permute-start(f32[32,768]{1,0:T(8,128)S(1)} %collective-permute-done.6.refs_2_), channel_id=1, source_target_pairs={{0,192},{1,65},{2,194},{3,67},{4,196},{5,69},{6,198},{7,71},{8,200... | collective-permute-start | bytes 294920 | tf_op jit(solution)/shard_map/ppermute | solution.py:371
  293.7 6.7 %collective-permute-start.19 = (f32[32,768]{1,0:T(8,128)S(1)}, f32[32,768]{1,0:T(8,128)S(1)}, u32[]{:S(2)}, u32[]{:S(2)}) collective-permute-start(f32[32,768]{1,0:T(8,128)S(1)} %mean.3.refs_3_), channel_id=1, source_target_pairs={{0,56},{1,9},{2,58},{3,11},{4,60},{5,13},{6,62},{7,15},{8,16},{9,1... | collective-permute-start | bytes 294920 | tf_op jit(solution)/shard_map/ppermute | solution.py:371
  294.5 8.0 %collective-permute-start.18 = (f32[32,768]{1,0:T(8,128)S(1)}, f32[32,768]{1,0:T(8,128)S(1)}, u32[]{:S(2)}, u32[]{:S(2)}) collective-permute-start(f32[32,768]{1,0:T(8,128)S(1)} %collective-permute-done.17.refs_2_), channel_id=1, source_target_pairs={{0,56},{1,9},{2,58},{3,11},{4,60},{5,13},{6,62},{7,15},{8,16},{9,1... | collective-permute-start | bytes 294920 | tf_op jit(solution)/shard_map/ppermute | solution.py:371
  298.3 7.9 %collective-permute-start.9 = (f32[128,768]{1,0:T(8,128)S(1)}, f32[128,768]{1,0:T(8,128)S(1)}, u32[]{:S(2)}, u32[]{:S(2)}) collective-permute-start(f32[128,768]{1,0:T(8,128)S(1)} %join.2.refs_0_), channel_id=1, source_target_pairs={{0,8},{1,57},{2,10},{3,59},{4,12},{5,61},{6,14},{7,63},{8,0},{9,17... | collective-permute-start | bytes 1179656 | tf_op jit(solution)/shard_map/ppermute | solution.py:371
  302.6 7.9 %collective-permute-start.20 = (f32[128,768]{1,0:T(8,128)S(1)}, f32[128,768]{1,0:T(8,128)S(1)}, u32[]{:S(2)}, u32[]{:S(2)}) collective-permute-start(f32[128,768]{1,0:T(8,128)S(1)} %join.3.refs_1_), channel_id=1, source_target_pairs={{0,64},{1,193},{2,66},{3,195},{4,68},{5,197},{6,70},{7,199},{8,72}... | collective-permute-start | bytes 1179656 | tf_op jit(solution)/shard_map/ppermute | solution.py:371
  302.7 12.0 %collective-permute-start.22 = (f32[128,768]{1,0:T(8,128)S(1)}, f32[128,768]{1,0:T(8,128)S(1)}, u32[]{:S(2)}, u32[]{:S(2)}) collective-permute-start(f32[128,768]{1,0:T(8,128)S(1)} %join.2.refs_0_), channel_id=1, source_target_pairs={{0,64},{1,193},{2,66},{3,195},{4,68},{5,197},{6,70},{7,199},{8,72}... | collective-permute-start | bytes 1179656 | tf_op jit(solution)/shard_map/ppermute | solution.py:371
  304.7 10.0 %collective-permute-start.23 = (f32[128,768]{1,0:T(8,128)S(1)}, f32[128,768]{1,0:T(8,128)S(1)}, u32[]{:S(2)}, u32[]{:S(2)}) collective-permute-start(f32[128,768]{1,0:T(8,128)S(1)} %join.3.refs_1_), channel_id=1, source_target_pairs={{0,8},{1,57},{2,10},{3,59},{4,12},{5,61},{6,14},{7,63},{8,0},{9,17... | collective-permute-start | bytes 1179656 | tf_op jit(solution)/shard_map/ppermute | solution.py:371
  306.2 12.7 %collective-permute-start.10 = (f32[128,768]{1,0:T(8,128)S(1)}, f32[128,768]{1,0:T(8,128)S(1)}, u32[]{:S(2)}, u32[]{:S(2)}) collective-permute-start(f32[128,768]{1,0:T(8,128)S(1)} %collective-permute-done.9.refs_2_), channel_id=1, source_target_pairs={{0,64},{1,193},{2,66},{3,195},{4,68},{5,197},{6,70},{7,199},{8,72}... | collective-permute-start | bytes 1179656 | tf_op jit(solution)/shard_map/ppermute | solution.py:371
  310.5 8.4 %collective-permute-start.21 = (f32[128,768]{1,0:T(8,128)S(1)}, f32[128,768]{1,0:T(8,128)S(1)}, u32[]{:S(2)}, u32[]{:S(2)}) collective-permute-start(f32[128,768]{1,0:T(8,128)S(1)} %collective-permute-done.20.refs_3_), channel_id=1, source_target_pairs={{0,8},{1,57},{2,10},{3,59},{4,12},{5,61},{6,14},{7,63},{8,0},{9,17... | collective-permute-start | bytes 1179656 | tf_op jit(solution)/shard_map/ppermute | solution.py:371
where the time goes:
time: 320 us
  Pallas kernels  175 us (55%)
  blocking collectives  82 us (26%)
  waiting for transfers between devices  36.5 us (11%)
  starting transfers between devices  25.6 us (8%)
    pallas_call x3, Pallas kernels, per_device(): pl.pallas_call(functools.partial(row_kernel, log_target), out_shape=row_p...  91 us
    all_to_all x3, blocking collectives, per_device(): col_got = lax.all_to_all(part, 'rows', 0, 0, tiled=True)  49.1 us
    pallas_call x1, Pallas kernels, per_device(): pl.pallas_call(logits_kernel, out_shape=(kept, peak_type, row_parts), in_...  40.4 us
    ppermute x24, waiting for transfers between devices, exchange(): lax.ppermute(x, ('rows', 'cols'), pairs(partner, lax.axis_size('cols')))  36.5 us
    all_to_all x4, blocking collectives, per_device(): row_got = lax.all_to_all(part, 'cols', 0, 0, tiled=True)  32.9 us
    pallas_call x3, Pallas kernels, per_device(): pl.pallas_call(col_kernel, out_shape=col_parts, in_specs=[vmem(), vmem(),...  28.2 us
    ppermute x24, starting transfers between devices, exchange(): lax.ppermute(x, ('rows', 'cols'), pairs(partner, lax.axis_size('cols')))  25.6 us
    pallas_call x4, Pallas kernels, quarter_sums(): pl.pallas_call(functools.partial(sums_kernel, log_target if first else No...  11.9 us
  transfers between devices with their start and end apart: 24, of which 16 were waited for; matrix products, arithmetic and copies ran while one was open for 0% of the time, Pallas kernels for 3%

commit v1 on v0

--- a/solution.py
+++ b/solution.py
@@ -498,7 +498,8 @@
     near = ((0, (False, False)), (1, (False, False)), (0, (False, True)), (1, (False, True)))
     out = put(near, (mine_a, mine_b, next_a, next_b), cents)
     out = put(((0, (True, False)), (1, (True, False))), (stay_a, stay_b), cents, out)
-    return put(((0, (True, True)), (1, (True, True))), (pass_a, pass_b), cents, out)
+    out = put(((0, (True, True)),), (pass_a,), cents, out)
+    return put(((1, (True, True)),), (pass_b,), cents, out)
 
 
 def vmem():

time: 320 us -> 321 us (level)
  transfers between devices with their start and end apart: 24 -> 24, of which waited for: 16 -> 16; matrix products, arithmetic and copies ran while one was open for 0% -> 0% of each run, Pallas kernels for 3% -> 4%
where the time goes in v1:
time: 321 us
  Pallas kernels  176 us (55%)
  blocking collectives  82 us (26%)
  waiting for transfers between devices  36.7 us (11%)
  starting transfers between devices  25.6 us (8%)
    pallas_call x3, Pallas kernels, per_device(): pl.pallas_call(functools.partial(row_kernel, log_target), out_shape=row_p...  91 us
    all_to_all x3, blocking collectives, per_device(): col_got = lax.all_to_all(part, 'rows', 0, 0, tiled=True)  49.1 us
    pallas_call x1, Pallas kernels, per_device(): pl.pallas_call(logits_kernel, out_shape=(kept, peak_type, row_parts), in_...  40.4 us
    ppermute x24, waiting for transfers between devices, exchange(): lax.ppermute(x, ('rows', 'cols'), pairs(partner, lax.axis_size('cols')))  36.7 us
    all_to_all x4, blocking collectives, per_device(): row_got = lax.all_to_all(part, 'cols', 0, 0, tiled=True)  32.9 us
    pallas_call x3, Pallas kernels, per_device(): pl.pallas_call(col_kernel, out_shape=col_parts, in_specs=[vmem(), vmem(),...  28.2 us
    ppermute x24, starting transfers between devices, exchange(): lax.ppermute(x, ('rows', 'cols'), pairs(partner, lax.axis_size('cols')))  25.6 us
    pallas_call x4, Pallas kernels, quarter_sums(): pl.pallas_call(functools.partial(sums_kernel, log_target if first else No...  11.9 us
  transfers between devices with their start and end apart: 24, of which 16 were waited for; matrix products, arithmetic and copies ran while one was open for 0% of the time, Pallas kernels for 4%

profile of v1, /device:TPU:8, one launch (start us, length us, event | category | flops | bytes accessed | tf_op | source)
XLA Modules:
  0.0 320.8 jit_solution(4413828447265445912)
XLA Ops:
  0.6 40.4 %logits.1 = (f32[1024,2048]{1,0:T(8,128)S(1)}, f32[8,128]{1,0:T(8,128)S(1)}, f32[8,16,128]{2,1,0:T(8,128)S(1)}) custom-call(bf16[1024,768]{1,0:T(8,128)(2,1)} %cent_hbm.1, bf16[2048,768]{1,0:T(8,128)(2,1)} %refs_4_.7), custom_call_target="tpu_custom_call" | custom-call | tf_op jit(solution)/shard_map/logits/pallas_call | solution.py:534
  41.0 8.9 %all_to_all.35.got_ref = f32[8,16,128]{2,1,0:T(8,128)S(1)} all-to-all(f32[8,16,128]{2,1,0:T(8,128)S(1)} %get-tuple-element.22), channel_id=1, replica_groups=mesh['rows'=32,'cols'=8] {'cols'}, dimensions={0} | all-to-all | bytes 131072 | tf_op jit(solution)/shard_map/all_to_all | solution.py:550
  49.9 9.4 %col_step.3 = f32[32,8,128]{2,1,0:T(8,128)S(1)} custom-call(f32[8,16,128]{2,1,0:T(8,128)S(1)} %all_to_all.35.got_ref, f32[8,128]{1,0:T(8,128)S(1)} %get-tuple-element.23.peak_ref.refs_2_, f32[1024,2048]{1,0:T(8,128)S(1)} %get-tuple-element.24.k_ref.refs_3_), custom_call_target="tpu_custom_call" | custom-call | tf_op jit(solution)/shard_map/col_step/pallas_call | solution.py:551
  59.3 21.4 %all_to_all.36.got_ref = f32[32,8,128]{2,1,0:T(8,128)S(1)} all-to-all(f32[32,8,128]{2,1,0:T(8,128)S(1)} %col_step.3), channel_id=1, replica_groups=mesh['rows'=32,'cols'=8] {'rows'}, dimensions={0} | all-to-all | bytes 262144 | tf_op jit(solution)/shard_map/all_to_all | solution.py:560
  80.6 30.3 %row_step.3 = f32[8,16,128]{2,1,0:T(8,128)S(1)} custom-call(f32[32,8,128]{2,1,0:T(8,128)S(1)} %all_to_all.36.got_ref, f32[8,128]{1,0:T(8,128)S(1)} %get-tuple-element.23.peak_ref.refs_2_, f32[1024,2048]{1,0:T(8,128)S(1)} %get-tuple-element.24.k_ref.refs_3_), custom_call_target="tpu_custom_call" | custom-call | tf_op jit(solution)/shard_map/row_step/pallas_call | solution.py:561
  111.0 8.0 %all_to_all.37.got_ref = f32[8,16,128]{2,1,0:T(8,128)S(1)} all-to-all(f32[8,16,128]{2,1,0:T(8,128)S(1)} %row_step.3), channel_id=1, replica_groups=mesh['rows'=32,'cols'=8] {'cols'}, dimensions={0} | all-to-all | bytes 131072 | tf_op jit(solution)/shard_map/all_to_all | solution.py:550
  119.0 9.4 %col_step.4 = f32[32,8,128]{2,1,0:T(8,128)S(1)} custom-call(f32[8,16,128]{2,1,0:T(8,128)S(1)} %all_to_all.37.got_ref, f32[8,128]{1,0:T(8,128)S(1)} %get-tuple-element.23.peak_ref.refs_2_, f32[1024,2048]{1,0:T(8,128)S(1)} %get-tuple-element.24.k_ref.refs_3_), custom_call_target="tpu_custom_call" | custom-call | tf_op jit(solution)/shard_map/col_step/pallas_call | solution.py:551
  128.4 13.9 %all_to_all.38.got_ref = f32[32,8,128]{2,1,0:T(8,128)S(1)} all-to-all(f32[32,8,128]{2,1,0:T(8,128)S(1)} %col_step.4), channel_id=1, replica_groups=mesh['rows'=32,'cols'=8] {'rows'}, dimensions={0} | all-to-all | bytes 262144 | tf_op jit(solution)/shard_map/all_to_all | solution.py:560
  142.2 30.3 %row_step.4 = f32[8,16,128]{2,1,0:T(8,128)S(1)} custom-call(f32[32,8,128]{2,1,0:T(8,128)S(1)} %all_to_all.38.got_ref, f32[8,128]{1,0:T(8,128)S(1)} %get-tuple-element.23.peak_ref.refs_2_, f32[1024,2048]{1,0:T(8,128)S(1)} %get-tuple-element.24.k_ref.refs_3_), custom_call_target="tpu_custom_call" | custom-call | tf_op jit(solution)/shard_map/row_step/pallas_call | solution.py:561
  172.6 8.0 %all_to_all.39.got_ref = f32[8,16,128]{2,1,0:T(8,128)S(1)} all-to-all(f32[8,16,128]{2,1,0:T(8,128)S(1)} %row_step.4), channel_id=1, replica_groups=mesh['rows'=32,'cols'=8] {'cols'}, dimensions={0} | all-to-all | bytes 131072 | tf_op jit(solution)/shard_map/all_to_all | solution.py:550
  180.6 9.4 %col_step.5 = f32[32,8,128]{2,1,0:T(8,128)S(1)} custom-call(f32[8,16,128]{2,1,0:T(8,128)S(1)} %all_to_all.39.got_ref, f32[8,128]{1,0:T(8,128)S(1)} %get-tuple-element.23.peak_ref.refs_2_, f32[1024,2048]{1,0:T(8,128)S(1)} %get-tuple-element.24.k_ref.refs_3_), custom_call_target="tpu_custom_call" | custom-call | tf_op jit(solution)/shard_map/col_step/pallas_call | solution.py:551
  190.0 13.9 %all_to_all.40.got_ref.refs_0_ = f32[32,8,128]{2,1,0:T(8,128)S(1)} all-to-all(f32[32,8,128]{2,1,0:T(8,128)S(1)} %col_step.5), channel_id=1, replica_groups=mesh['rows'=32,'cols'=8] {'rows'}, dimensions={0} | all-to-all | bytes 262144 | tf_op jit(solution)/shard_map/all_to_all | solution.py:560
  203.8 30.3 %row_step.5 = f32[8,16,128]{2,1,0:T(8,128)S(1)} custom-call(f32[32,8,128]{2,1,0:T(8,128)S(1)} %all_to_all.40.got_ref.refs_0_, f32[8,128]{1,0:T(8,128)S(1)} %get-tuple-element.23.peak_ref.refs_2_, f32[1024,2048]{1,0:T(8,128)S(1)} %get-tuple-element.24.k_ref.refs_3_), custom_call_target="tpu_custom_call" | custom-call | tf_op jit(solution)/shard_map/row_step/pallas_call | solution.py:561
  234.1 8.0 %all_to_all.41.refs_1_ = f32[8,16,128]{2,1,0:T(8,128)S(1)} all-to-all(f32[8,16,128]{2,1,0:T(8,128)S(1)} %row_step.5), channel_id=1, replica_groups=mesh['rows'=32,'cols'=8] {'cols'}, dimensions={0} | all-to-all | bytes 131072 | tf_op jit(solution)/shard_map/all_to_all | solution.py:570
  242.1 3.3 %sums.4 = (f32[4,25,8,128]{3,2,1,0:T(8,128)S(1)}, f32[4,25,8,128]{3,2,1,0:T(8,128)S(1)}, f32[8,128]{1,0:T(8,128)}, f32[8,128]{1,0:T(8,128)S(1)}, f32[16,128]{1,0:T(8,128)}, /*index=5*/f32[16,128]{1,0:T(8,128)S(1)}) custom-call(f32[32,8,128]{2,1,0:T(8,128)S(1)} %all_to_all.40.got_ref.refs_0_, f32[8,16,128]{2,1,0:T(8,128)S(1)} %all_to_all.41.refs_1_, ...), custom_call_target="tpu_custom_call" | custom-call | flops 805306368 | bytes 4194304 | tf_op jit(solution)/shard_map/sums/pallas_call | solution.py:578
  245.4 0.6 collective-permute-start.12
  246.1 1.3 collective-permute-start.1
  247.3 2.9 sums.6
  250.2 1.5 collective-permute-start.11
  251.7 2.9 sums.7
  254.6 0.9 collective-permute-start.13
  255.5 1.3 collective-permute-start
  256.8 0.7 collective-permute-start.2
  257.5 2.9 sums.5
  260.4 2.3 collective-permute-done.13.second_ref
  262.6 0.1 pieces.3
  262.7 1.3 collective-permute-start.14
  264.0 3.1 collective-permute-done.first_ref
  267.0 0.1 pieces.2
  267.1 0.7 collective-permute-start.3
  267.8 2.0 collective-permute-done.14.got_ref
  269.8 0.8 collective-permute-start.15
  270.5 3.6 %collective-permute-done.3.got_ref = f32[2,25,8,128]{3,2,1,0:T(8,128)S(1)} collective-permute-done((f32[2,25,8,128]{3,2,1,0:T(8,128)S(1)}, f32[2,25,8,128]{3,2,1,0:T(8,128)S(1)}, u32[]{:S(2)}, u32[]{:S(2)}) %collective-permute-start.3) | collective-permute-done | bytes 204832 | tf_op jit(solution)/shard_map/ppermute | solution.py:371
  274.2 1.3 collective-permute-start.4
  275.4 0.3 collective-permute-done.15.second_ref
  275.8 1.6 collective-permute-start.16
  277.4 2.7 collective-permute-done.4.second_ref
  280.2 1.6 collective-permute-start.5
  281.8 3.6 %collective-permute-done.16.got_ref = f32[25,8,128]{2,1,0:T(8,128)S(1)} collective-permute-done((f32[25,8,128]{2,1,0:T(8,128)S(1)}, f32[25,8,128]{2,1,0:T(8,128)S(1)}, u32[]{:S(2)}, u32[]{:S(2)}) %collective-permute-start.16) | collective-permute-done | bytes 102432 | tf_op jit(solution)/shard_map/ppermute | solution.py:371
  285.4 0.1 mean.3.refs_3_
  285.5 0.1 collective-permute-start.17
  285.6 1.8 collective-permute-done.5.got_ref
  287.4 0.1 mean.2.refs_3_
  287.4 2.0 collective-permute-start.6
  289.5 1.3 collective-permute-start.19
  290.8 0.6 collective-permute-done.17.refs_2_
  291.4 2.3 collective-permute-start.18
  293.7 0.8 collective-permute-start.8
  294.5 2.4 collective-permute-start.7
  297.0 1.3 collective-permute-done.18.refs_0_
  298.3 1.1 collective-permute-start.20
  299.4 1.2 collective-permute-done.8.refs_1_
  300.7 2.1 collective-permute-done.7.refs_0_
  302.8 0.1 collective-permute-start.9
  302.9 0.1 collective-permute-start.23
  303.0 1.9 collective-permute-start.22
  304.9 1.3 collective-permute-done.20.refs_2_
  306.2 4.5 %collective-permute-done.9.refs_3_ = f32[128,768]{1,0:T(8,128)S(1)} collective-permute-done((f32[128,768]{1,0:T(8,128)S(1)}, f32[128,768]{1,0:T(8,128)S(1)}, u32[]{:S(2)}, u32[]{:S(2)}) %collective-permute-start.9) | collective-permute-done | bytes 393248 | tf_op jit(solution)/shard_map/ppermute | solution.py:371
  310.7 1.2 place.4.refs_2_
  311.9 3.0 collective-permute-done.22.refs_0_
  314.9 0.9 place.5.refs_1_
  315.8 3.3 %collective-permute-done.21.refs_0_ = f32[128,768]{1,0:T(8,128)S(1)} collective-permute-done((f32[128,768]{1,0:T(8,128)S(1)}, f32[128,768]{1,0:T(8,128)S(1)}, u32[]{:S(2)}, u32[]{:S(2)}) %collective-permute-start.21) | collective-permute-done | bytes 393248 | tf_op jit(solution)/shard_map/ppermute | solution.py:371
  319.1 0.8 place.6.refs_1_
  319.9 0.8 place.7
  (20 shorter events, 0.3 us)
Async XLA Ops:
  203.8 38.3 %copy-start = (bf16[2048,768]{1,0:T(8,128)(2,1)S(1)}, bf16[2048,768]{1,0:T(8,128)(2,1)}, u32[]{:S(2)}) copy-start(bf16[2048,768]{1,0:T(8,128)(2,1)} %refs_4_.7) | copy-start | bytes 9437188
  245.4 9.1 %collective-permute-start.12 = (f32[4,25,8,128]{3,2,1,0:T(8,128)S(1)}, f32[4,25,8,128]{3,2,1,0:T(8,128)S(1)}, u32[]{:S(2)}, u32[]{:S(2)}) collective-permute-start(f32[4,25,8,128]{3,2,1,0:T(8,128)S(1)} %get-tuple-element.36), channel_id=1, source_target_pairs={{0,64},{1,193},{2,66},{3,195},{4,68},{5,197},{6,70},{7,199},{8,72}... | collective-permute-start | bytes 1228808 | tf_op jit(solution)/shard_map/ppermute | solution.py:371
  246.1 10.7 %collective-permute-start.1 = (f32[4,25,8,128]{3,2,1,0:T(8,128)S(1)}, f32[4,25,8,128]{3,2,1,0:T(8,128)S(1)}, u32[]{:S(2)}, u32[]{:S(2)}) collective-permute-start(f32[4,25,8,128]{3,2,1,0:T(8,128)S(1)} %get-tuple-element.30), channel_id=1, source_target_pairs={{0,8},{1,57},{2,10},{3,59},{4,12},{5,61},{6,14},{7,63},{8,0},{9,17... | collective-permute-start | bytes 1228808 | tf_op jit(solution)/shard_map/ppermute | solution.py:371
  250.2 10.2 %collective-permute-start.11 = (f32[4,25,8,128]{3,2,1,0:T(8,128)S(1)}, f32[4,25,8,128]{3,2,1,0:T(8,128)S(1)}, u32[]{:S(2)}, u32[]{:S(2)}) collective-permute-start(f32[4,25,8,128]{3,2,1,0:T(8,128)S(1)} %get-tuple-element.34), channel_id=1, source_target_pairs={{0,64},{1,193},{2,66},{3,195},{4,68},{5,197},{6,70},{7,199},{8,72}... | collective-permute-start | bytes 1228808 | tf_op jit(solution)/shard_map/ppermute | solution.py:371
  254.6 8.0 %collective-permute-start.13 = (f32[4,25,8,128]{3,2,1,0:T(8,128)S(1)}, f32[4,25,8,128]{3,2,1,0:T(8,128)S(1)}, u32[]{:S(2)}, u32[]{:S(2)}) collective-permute-start(f32[4,25,8,128]{3,2,1,0:T(8,128)S(1)} %add.3), channel_id=1, source_target_pairs={{0,8},{1,57},{2,10},{3,59},{4,12},{5,61},{6,14},{7,63},{8,0},{9,17... | collective-permute-start | bytes 1228808 | tf_op jit(solution)/shard_map/ppermute | solution.py:371
  255.5 11.6 %collective-permute-start = (f32[4,25,8,128]{3,2,1,0:T(8,128)S(1)}, f32[4,25,8,128]{3,2,1,0:T(8,128)S(1)}, u32[]{:S(2)}, u32[]{:S(2)}) collective-permute-start(f32[4,25,8,128]{3,2,1,0:T(8,128)S(1)} %get-tuple-element.28), channel_id=1, source_target_pairs={{0,8},{1,57},{2,10},{3,59},{4,12},{5,61},{6,14},{7,63},{8,0},{9,17... | collective-permute-start | bytes 1228808 | tf_op jit(solution)/shard_map/ppermute | solution.py:371
  256.8 10.3 %collective-permute-start.2 = (f32[4,25,8,128]{3,2,1,0:T(8,128)S(1)}, f32[4,25,8,128]{3,2,1,0:T(8,128)S(1)}, u32[]{:S(2)}, u32[]{:S(2)}) collective-permute-start(f32[4,25,8,128]{3,2,1,0:T(8,128)S(1)} %add.2), channel_id=1, source_target_pairs={{0,64},{1,193},{2,66},{3,195},{4,68},{5,197},{6,70},{7,199},{8,72}... | collective-permute-start | bytes 1228808 | tf_op jit(solution)/shard_map/ppermute | solution.py:371
  262.7 7.1 %collective-permute-start.14 = (f32[2,25,8,128]{3,2,1,0:T(8,128)S(1)}, f32[2,25,8,128]{3,2,1,0:T(8,128)S(1)}, u32[]{:S(2)}, u32[]{:S(2)}) collective-permute-start(f32[2,25,8,128]{3,2,1,0:T(8,128)S(1)} %get-tuple-element.38), channel_id=1, source_target_pairs={{0,192},{1,65},{2,194},{3,67},{4,196},{5,69},{6,198},{7,71},{8,200... | collective-permute-start | bytes 614408 | tf_op jit(solution)/shard_map/ppermute | solution.py:371
  267.1 7.1 %collective-permute-start.3 = (f32[2,25,8,128]{3,2,1,0:T(8,128)S(1)}, f32[2,25,8,128]{3,2,1,0:T(8,128)S(1)}, u32[]{:S(2)}, u32[]{:S(2)}) collective-permute-start(f32[2,25,8,128]{3,2,1,0:T(8,128)S(1)} %get-tuple-element.32), channel_id=1, source_target_pairs={{0,56},{1,9},{2,58},{3,11},{4,60},{5,13},{6,62},{7,15},{8,16},{9,1... | collective-permute-start | bytes 614408 | tf_op jit(solution)/shard_map/ppermute | solution.py:371
  269.8 6.0 %collective-permute-start.15 = (f32[25,8,128]{2,1,0:T(8,128)S(1)}, f32[25,8,128]{2,1,0:T(8,128)S(1)}, u32[]{:S(2)}, u32[]{:S(2)}) collective-permute-start(f32[25,8,128]{2,1,0:T(8,128)S(1)} %hold.3), channel_id=1, source_target_pairs={{0,56},{1,9},{2,58},{3,11},{4,60},{5,13},{6,62},{7,15},{8,16},{9,1... | collective-permute-start | bytes 307208 | tf_op jit(solution)/shard_map/ppermute | solution.py:371
  274.2 6.0 %collective-permute-start.4 = (f32[25,8,128]{2,1,0:T(8,128)S(1)}, f32[25,8,128]{2,1,0:T(8,128)S(1)}, u32[]{:S(2)}, u32[]{:S(2)}) collective-permute-start(f32[25,8,128]{2,1,0:T(8,128)S(1)} %hold.2), channel_id=1, source_target_pairs={{0,192},{1,65},{2,194},{3,67},{4,196},{5,69},{6,198},{7,71},{8,200... | collective-permute-start | bytes 307208 | tf_op jit(solution)/shard_map/ppermute | solution.py:371
  275.8 9.6 %collective-permute-start.16 = (f32[25,8,128]{2,1,0:T(8,128)S(1)}, f32[25,8,128]{2,1,0:T(8,128)S(1)}, u32[]{:S(2)}, u32[]{:S(2)}) collective-permute-start(f32[25,8,128]{2,1,0:T(8,128)S(1)} %own.3.sum_ref), channel_id=1, source_target_pairs={{0,24},{1,41},{2,26},{3,43},{4,28},{5,45},{6,30},{7,47},{8,48},{9,... | collective-permute-start | bytes 307208 | tf_op jit(solution)/shard_map/ppermute | solution.py:371
  280.2 7.2 %collective-permute-start.5 = (f32[25,8,128]{2,1,0:T(8,128)S(1)}, f32[25,8,128]{2,1,0:T(8,128)S(1)}, u32[]{:S(2)}, u32[]{:S(2)}) collective-permute-start(f32[25,8,128]{2,1,0:T(8,128)S(1)} %own.2.sum_ref), channel_id=1, source_target_pairs={{0,24},{1,41},{2,26},{3,43},{4,28},{5,45},{6,30},{7,47},{8,48},{9,... | collective-permute-start | bytes 307208 | tf_op jit(solution)/shard_map/ppermute | solution.py:371
  285.5 5.9 %collective-permute-start.17 = (f32[32,768]{1,0:T(8,128)S(1)}, f32[32,768]{1,0:T(8,128)S(1)}, u32[]{:S(2)}, u32[]{:S(2)}) collective-permute-start(f32[32,768]{1,0:T(8,128)S(1)} %mean.3.refs_3_), channel_id=1, source_target_pairs={{0,56},{1,9},{2,58},{3,11},{4,60},{5,13},{6,62},{7,15},{8,16},{9,1... | collective-permute-start | bytes 294920 | tf_op jit(solution)/shard_map/ppermute | solution.py:371
  287.4 7.1 %collective-permute-start.6 = (f32[32,768]{1,0:T(8,128)S(1)}, f32[32,768]{1,0:T(8,128)S(1)}, u32[]{:S(2)}, u32[]{:S(2)}) collective-permute-start(f32[32,768]{1,0:T(8,128)S(1)} %mean.2.refs_3_), channel_id=1, source_target_pairs={{0,192},{1,65},{2,194},{3,67},{4,196},{5,69},{6,198},{7,71},{8,200... | collective-permute-start | bytes 294920 | tf_op jit(solution)/shard_map/ppermute | solution.py:371
  289.5 7.5 %collective-permute-start.19 = (f32[32,768]{1,0:T(8,128)S(1)}, f32[32,768]{1,0:T(8,128)S(1)}, u32[]{:S(2)}, u32[]{:S(2)}) collective-permute-start(f32[32,768]{1,0:T(8,128)S(1)} %mean.3.refs_3_), channel_id=1, source_target_pairs={{0,192},{1,65},{2,194},{3,67},{4,196},{5,69},{6,198},{7,71},{8,200... | collective-permute-start | bytes 294920 | tf_op jit(solution)/shard_map/ppermute | solution.py:371
  291.4 6.9 %collective-permute-start.18 = (f32[32,768]{1,0:T(8,128)S(1)}, f32[32,768]{1,0:T(8,128)S(1)}, u32[]{:S(2)}, u32[]{:S(2)}) collective-permute-start(f32[32,768]{1,0:T(8,128)S(1)} %collective-permute-done.17.refs_2_), channel_id=1, source_target_pairs={{0,192},{1,65},{2,194},{3,67},{4,196},{5,69},{6,198},{7,71},{8,200... | collective-permute-start | bytes 294920 | tf_op jit(solution)/shard_map/ppermute | solution.py:371
  293.7 6.9 %collective-permute-start.8 = (f32[32,768]{1,0:T(8,128)S(1)}, f32[32,768]{1,0:T(8,128)S(1)}, u32[]{:S(2)}, u32[]{:S(2)}) collective-permute-start(f32[32,768]{1,0:T(8,128)S(1)} %mean.2.refs_3_), channel_id=1, source_target_pairs={{0,56},{1,9},{2,58},{3,11},{4,60},{5,13},{6,62},{7,15},{8,16},{9,1... | collective-permute-start | bytes 294920 | tf_op jit(solution)/shard_map/ppermute | solution.py:371
  294.5 8.2 %collective-permute-start.7 = (f32[32,768]{1,0:T(8,128)S(1)}, f32[32,768]{1,0:T(8,128)S(1)}, u32[]{:S(2)}, u32[]{:S(2)}) collective-permute-start(f32[32,768]{1,0:T(8,128)S(1)} %collective-permute-done.6.refs_2_), channel_id=1, source_target_pairs={{0,56},{1,9},{2,58},{3,11},{4,60},{5,13},{6,62},{7,15},{8,16},{9,1... | collective-permute-start | bytes 294920 | tf_op jit(solution)/shard_map/ppermute | solution.py:371
  298.3 7.9 %collective-permute-start.20 = (f32[128,768]{1,0:T(8,128)S(1)}, f32[128,768]{1,0:T(8,128)S(1)}, u32[]{:S(2)}, u32[]{:S(2)}) collective-permute-start(f32[128,768]{1,0:T(8,128)S(1)} %join.3.refs_0_), channel_id=1, source_target_pairs={{0,8},{1,57},{2,10},{3,59},{4,12},{5,61},{6,14},{7,63},{8,0},{9,17... | collective-permute-start | bytes 1179656 | tf_op jit(solution)/shard_map/ppermute | solution.py:371
  302.8 7.9 %collective-permute-start.9 = (f32[128,768]{1,0:T(8,128)S(1)}, f32[128,768]{1,0:T(8,128)S(1)}, u32[]{:S(2)}, u32[]{:S(2)}) collective-permute-start(f32[128,768]{1,0:T(8,128)S(1)} %join.2.refs_1_), channel_id=1, source_target_pairs={{0,64},{1,193},{2,66},{3,195},{4,68},{5,197},{6,70},{7,199},{8,72}... | collective-permute-start | bytes 1179656 | tf_op jit(solution)/shard_map/ppermute | solution.py:371
  302.9 8.9 %collective-permute-start.23 = (f32[128,768]{1,0:T(8,128)S(1)}, f32[128,768]{1,0:T(8,128)S(1)}, u32[]{:S(2)}, u32[]{:S(2)}) collective-permute-start(f32[128,768]{1,0:T(8,128)S(1)} %join.2.refs_1_), channel_id=1, source_target_pairs={{0,8},{1,57},{2,10},{3,59},{4,12},{5,61},{6,14},{7,63},{8,0},{9,17... | collective-permute-start | bytes 1179656 | tf_op jit(solution)/shard_map/ppermute | solution.py:371
  303.0 11.9 %collective-permute-start.22 = (f32[128,768]{1,0:T(8,128)S(1)}, f32[128,768]{1,0:T(8,128)S(1)}, u32[]{:S(2)}, u32[]{:S(2)}) collective-permute-start(f32[128,768]{1,0:T(8,128)S(1)} %join.3.refs_0_), channel_id=1, source_target_pairs={{0,64},{1,193},{2,66},{3,195},{4,68},{5,197},{6,70},{7,199},{8,72}... | collective-permute-start | bytes 1179656 | tf_op jit(solution)/shard_map/ppermute | solution.py:371
  306.2 12.9 %collective-permute-start.21 = (f32[128,768]{1,0:T(8,128)S(1)}, f32[128,768]{1,0:T(8,128)S(1)}, u32[]{:S(2)}, u32[]{:S(2)}) collective-permute-start(f32[128,768]{1,0:T(8,128)S(1)} %collective-permute-done.20.refs_2_), channel_id=1, source_target_pairs={{0,64},{1,193},{2,66},{3,195},{4,68},{5,197},{6,70},{7,199},{8,72}... | collective-permute-start | bytes 1179656 | tf_op jit(solution)/shard_map/ppermute | solution.py:371
  310.7 9.2 %collective-permute-start.10 = (f32[128,768]{1,0:T(8,128)S(1)}, f32[128,768]{1,0:T(8,128)S(1)}, u32[]{:S(2)}, u32[]{:S(2)}) collective-permute-start(f32[128,768]{1,0:T(8,128)S(1)} %collective-permute-done.9.refs_3_), channel_id=1, source_target_pairs={{0,8},{1,57},{2,10},{3,59},{4,12},{5,61},{6,14},{7,63},{8,0},{9,17... | collective-permute-start | bytes 1179656 | tf_op jit(solution)/shard_map/ppermute | solution.py:371

commit v2 on v0

--- a/solution.py
+++ b/solution.py
@@ -17,7 +17,7 @@
 XS, ZS = 4, 8
 BLOCK = 32
 PARTS = BLOCK // 8
-CHUNKS = 4
+CHUNKS = 2
 XB1, XB2, ZB1, ZB2 = range(4)
 
 

time: 320 us -> 320 us (level)
  no operation moved by 1% of the time
where the time goes in v2:
time: 320 us; the launch traced here: 319 us
  Pallas kernels  174 us (54%)
  blocking collectives  82 us (26%)
  waiting for transfers between devices  36.7 us (11%)
  starting transfers between devices  25.4 us (8%)
    pallas_call x3, Pallas kernels, per_device(): pl.pallas_call(functools.partial(row_kernel, log_target), out_shape=row_p...  91 us
    all_to_all x3, blocking collectives, per_device(): col_got = lax.all_to_all(part, 'rows', 0, 0, tiled=True)  49.1 us
    pallas_call x1, Pallas kernels, per_device(): pl.pallas_call(logits_kernel, out_shape=(kept, peak_type, row_parts), in_...  39.8 us
    ppermute x24, waiting for transfers between devices, exchange(): lax.ppermute(x, ('rows', 'cols'), pairs(partner, lax.axis_size('cols')))  36.7 us
    all_to_all x4, blocking collectives, per_device(): row_got = lax.all_to_all(part, 'cols', 0, 0, tiled=True)  32.9 us
    pallas_call x3, Pallas kernels, per_device(): pl.pallas_call(col_kernel, out_shape=col_parts, in_specs=[vmem(), vmem(),...  28.2 us
    ppermute x24, starting transfers between devices, exchange(): lax.ppermute(x, ('rows', 'cols'), pairs(partner, lax.axis_size('cols')))  25.4 us
    pallas_call x4, Pallas kernels, quarter_sums(): pl.pallas_call(functools.partial(sums_kernel, log_target if first else No...  11.9 us
  transfers between devices with their start and end apart: 24, of which 16 were waited for; matrix products, arithmetic and copies ran while one was open for 0% of the time, Pallas kernels for 3%

profile of v2, /device:TPU:8, one launch (start us, length us, event | category | flops | bytes accessed | tf_op | source)
XLA Modules:
  0.0 319.5 jit_solution(10722783949687697405)
XLA Ops:
  0.6 39.8 %logits.1 = (f32[1024,2048]{1,0:T(8,128)S(1)}, f32[8,128]{1,0:T(8,128)S(1)}, f32[8,16,128]{2,1,0:T(8,128)S(1)}) custom-call(bf16[1024,768]{1,0:T(8,128)(2,1)} %cent_hbm.1, bf16[2048,768]{1,0:T(8,128)(2,1)} %refs_4_.7), custom_call_target="tpu_custom_call" | custom-call | tf_op jit(solution)/shard_map/logits/pallas_call | solution.py:533
  40.5 8.9 %all_to_all.35.got_ref = f32[8,16,128]{2,1,0:T(8,128)S(1)} all-to-all(f32[8,16,128]{2,1,0:T(8,128)S(1)} %get-tuple-element.22), channel_id=1, replica_groups=mesh['rows'=32,'cols'=8] {'cols'}, dimensions={0} | all-to-all | bytes 131072 | tf_op jit(solution)/shard_map/all_to_all | solution.py:549
  49.3 9.4 %col_step.3 = f32[32,8,128]{2,1,0:T(8,128)S(1)} custom-call(f32[8,16,128]{2,1,0:T(8,128)S(1)} %all_to_all.35.got_ref, f32[8,128]{1,0:T(8,128)S(1)} %get-tuple-element.23.peak_ref.refs_2_, f32[1024,2048]{1,0:T(8,128)S(1)} %get-tuple-element.24.k_ref.refs_3_), custom_call_target="tpu_custom_call" | custom-call | tf_op jit(solution)/shard_map/col_step/pallas_call | solution.py:550
  58.7 21.4 %all_to_all.36.got_ref = f32[32,8,128]{2,1,0:T(8,128)S(1)} all-to-all(f32[32,8,128]{2,1,0:T(8,128)S(1)} %col_step.3), channel_id=1, replica_groups=mesh['rows'=32,'cols'=8] {'rows'}, dimensions={0} | all-to-all | bytes 262144 | tf_op jit(solution)/shard_map/all_to_all | solution.py:559
  80.1 30.3 %row_step.3 = f32[8,16,128]{2,1,0:T(8,128)S(1)} custom-call(f32[32,8,128]{2,1,0:T(8,128)S(1)} %all_to_all.36.got_ref, f32[8,128]{1,0:T(8,128)S(1)} %get-tuple-element.23.peak_ref.refs_2_, f32[1024,2048]{1,0:T(8,128)S(1)} %get-tuple-element.24.k_ref.refs_3_), custom_call_target="tpu_custom_call" | custom-call | tf_op jit(solution)/shard_map/row_step/pallas_call | solution.py:560
  110.5 8.0 %all_to_all.37.got_ref = f32[8,16,128]{2,1,0:T(8,128)S(1)} all-to-all(f32[8,16,128]{2,1,0:T(8,128)S(1)} %row_step.3), channel_id=1, replica_groups=mesh['rows'=32,'cols'=8] {'cols'}, dimensions={0} | all-to-all | bytes 131072 | tf_op jit(solution)/shard_map/all_to_all | solution.py:549
  118.5 9.4 %col_step.4 = f32[32,8,128]{2,1,0:T(8,128)S(1)} custom-call(f32[8,16,128]{2,1,0:T(8,128)S(1)} %all_to_all.37.got_ref, f32[8,128]{1,0:T(8,128)S(1)} %get-tuple-element.23.peak_ref.refs_2_, f32[1024,2048]{1,0:T(8,128)S(1)} %get-tuple-element.24.k_ref.refs_3_), custom_call_target="tpu_custom_call" | custom-call | tf_op jit(solution)/shard_map/col_step/pallas_call | solution.py:550
  127.9 13.9 %all_to_all.38.got_ref = f32[32,8,128]{2,1,0:T(8,128)S(1)} all-to-all(f32[32,8,128]{2,1,0:T(8,128)S(1)} %col_step.4), channel_id=1, replica_groups=mesh['rows'=32,'cols'=8] {'rows'}, dimensions={0} | all-to-all | bytes 262144 | tf_op jit(solution)/shard_map/all_to_all | solution.py:559
  141.7 30.3 %row_step.4 = f32[8,16,128]{2,1,0:T(8,128)S(1)} custom-call(f32[32,8,128]{2,1,0:T(8,128)S(1)} %all_to_all.38.got_ref, f32[8,128]{1,0:T(8,128)S(1)} %get-tuple-element.23.peak_ref.refs_2_, f32[1024,2048]{1,0:T(8,128)S(1)} %get-tuple-element.24.k_ref.refs_3_), custom_call_target="tpu_custom_call" | custom-call | tf_op jit(solution)/shard_map/row_step/pallas_call | solution.py:560
  172.0 8.0 %all_to_all.39.got_ref = f32[8,16,128]{2,1,0:T(8,128)S(1)} all-to-all(f32[8,16,128]{2,1,0:T(8,128)S(1)} %row_step.4), channel_id=1, replica_groups=mesh['rows'=32,'cols'=8] {'cols'}, dimensions={0} | all-to-all | bytes 131072 | tf_op jit(solution)/shard_map/all_to_all | solution.py:549
  180.0 9.4 %col_step.5 = f32[32,8,128]{2,1,0:T(8,128)S(1)} custom-call(f32[8,16,128]{2,1,0:T(8,128)S(1)} %all_to_all.39.got_ref, f32[8,128]{1,0:T(8,128)S(1)} %get-tuple-element.23.peak_ref.refs_2_, f32[1024,2048]{1,0:T(8,128)S(1)} %get-tuple-element.24.k_ref.refs_3_), custom_call_target="tpu_custom_call" | custom-call | tf_op jit(solution)/shard_map/col_step/pallas_call | solution.py:550
  189.4 13.9 %all_to_all.40.got_ref.refs_0_ = f32[32,8,128]{2,1,0:T(8,128)S(1)} all-to-all(f32[32,8,128]{2,1,0:T(8,128)S(1)} %col_step.5), channel_id=1, replica_groups=mesh['rows'=32,'cols'=8] {'rows'}, dimensions={0} | all-to-all | bytes 262144 | tf_op jit(solution)/shard_map/all_to_all | solution.py:559
  203.3 30.3 %row_step.5 = f32[8,16,128]{2,1,0:T(8,128)S(1)} custom-call(f32[32,8,128]{2,1,0:T(8,128)S(1)} %all_to_all.40.got_ref.refs_0_, f32[8,128]{1,0:T(8,128)S(1)} %get-tuple-element.23.peak_ref.refs_2_, f32[1024,2048]{1,0:T(8,128)S(1)} %get-tuple-element.24.k_ref.refs_3_), custom_call_target="tpu_custom_call" | custom-call | tf_op jit(solution)/shard_map/row_step/pallas_call | solution.py:560
  233.6 8.0 %all_to_all.41.refs_1_ = f32[8,16,128]{2,1,0:T(8,128)S(1)} all-to-all(f32[8,16,128]{2,1,0:T(8,128)S(1)} %row_step.5), channel_id=1, replica_groups=mesh['rows'=32,'cols'=8] {'cols'}, dimensions={0} | all-to-all | bytes 131072 | tf_op jit(solution)/shard_map/all_to_all | solution.py:569
  241.6 3.3 %sums.4 = (f32[4,25,8,128]{3,2,1,0:T(8,128)S(1)}, f32[4,25,8,128]{3,2,1,0:T(8,128)S(1)}, f32[8,128]{1,0:T(8,128)}, f32[8,128]{1,0:T(8,128)S(1)}, f32[16,128]{1,0:T(8,128)}, /*index=5*/f32[16,128]{1,0:T(8,128)S(1)}) custom-call(f32[32,8,128]{2,1,0:T(8,128)S(1)} %all_to_all.40.got_ref.refs_0_, f32[8,16,128]{2,1,0:T(8,128)S(1)} %all_to_all.41.refs_1_, ...), custom_call_target="tpu_custom_call" | custom-call | flops 805306368 | bytes 4194304 | tf_op jit(solution)/shard_map/sums/pallas_call | solution.py:577
  244.9 0.6 collective-permute-start.1
  245.5 1.3 collective-permute-start.12
  246.8 2.9 sums.6
  249.7 1.5 collective-permute-start
  251.1 2.9 sums.7
  254.1 0.9 collective-permute-start.2
  254.9 1.3 collective-permute-start.11
  256.2 0.0 collective-permute-done.12.got_ref
  256.2 0.7 collective-permute-start.13
  257.0 2.9 sums.5
  259.8 0.0 collective-permute-done.first_ref
  259.8 2.3 collective-permute-done.2.second_ref
  262.1 0.1 pieces.2
  262.2 1.3 collective-permute-start.3
  263.4 3.1 collective-permute-done.11.first_ref
  266.5 0.1 pieces.3
  266.6 0.7 collective-permute-start.14
  267.3 2.0 collective-permute-done.3.got_ref
  269.3 0.8 collective-permute-start.4
  270.0 3.6 %collective-permute-done.14.got_ref = f32[2,25,8,128]{3,2,1,0:T(8,128)S(1)} collective-permute-done((f32[2,25,8,128]{3,2,1,0:T(8,128)S(1)}, f32[2,25,8,128]{3,2,1,0:T(8,128)S(1)}, u32[]{:S(2)}, u32[]{:S(2)}) %collective-permute-start.14) | collective-permute-done | bytes 204832 | tf_op jit(solution)/shard_map/ppermute | solution.py:371
  273.7 1.3 collective-permute-start.15
  274.9 0.3 collective-permute-done.4.second_ref
  275.2 1.6 collective-permute-start.5
  276.9 2.7 collective-permute-done.15.second_ref
  279.6 1.6 collective-permute-start.16
  281.3 3.6 %collective-permute-done.5.got_ref = f32[25,8,128]{2,1,0:T(8,128)S(1)} collective-permute-done((f32[25,8,128]{2,1,0:T(8,128)S(1)}, f32[25,8,128]{2,1,0:T(8,128)S(1)}, u32[]{:S(2)}, u32[]{:S(2)}) %collective-permute-start.5) | collective-permute-done | bytes 102432 | tf_op jit(solution)/shard_map/ppermute | solution.py:371
  284.9 0.1 mean.2.refs_3_
  285.0 0.1 collective-permute-start.6
  285.1 1.8 collective-permute-done.16.got_ref
  286.8 0.1 mean.3.refs_3_
  286.9 2.0 collective-permute-start.17
  289.0 1.3 collective-permute-start.8
  290.2 0.6 collective-permute-done.6.refs_2_
  290.9 2.3 collective-permute-start.7
  293.2 0.8 collective-permute-start.19
  294.0 2.4 collective-permute-start.18
  296.4 1.3 collective-permute-done.7.refs_0_
  297.8 0.9 collective-permute-start.9
  298.7 1.2 collective-permute-done.19.refs_1_
  299.9 2.1 collective-permute-done.18.refs_0_
  302.1 0.1 collective-permute-start.20
  302.2 2.0 collective-permute-start.22
  304.2 1.5 collective-permute-done.9.refs_2_
  305.7 4.3 %collective-permute-done.20.refs_3_ = f32[128,768]{1,0:T(8,128)S(1)} collective-permute-done((f32[128,768]{1,0:T(8,128)S(1)}, f32[128,768]{1,0:T(8,128)S(1)}, u32[]{:S(2)}, u32[]{:S(2)}) %collective-permute-start.20) | collective-permute-done | bytes 393248 | tf_op jit(solution)/shard_map/ppermute | solution.py:371
  310.0 1.2 place.3.refs_2_
  311.1 3.0 collective-permute-done.22.refs_0_
  314.2 0.9 place.4.refs_2_
  315.1 3.3 %collective-permute-done.10.refs_0_ = f32[128,768]{1,0:T(8,128)S(1)} collective-permute-done((f32[128,768]{1,0:T(8,128)S(1)}, f32[128,768]{1,0:T(8,128)S(1)}, u32[]{:S(2)}, u32[]{:S(2)}) %collective-permute-start.10) | collective-permute-done | bytes 393248 | tf_op jit(solution)/shard_map/ppermute | solution.py:371
  318.4 0.9 place.5
  (19 shorter events, 0.3 us)
Async XLA Ops:
  203.3 38.3 %copy-start = (bf16[2048,768]{1,0:T(8,128)(2,1)S(1)}, bf16[2048,768]{1,0:T(8,128)(2,1)}, u32[]{:S(2)}) copy-start(bf16[2048,768]{1,0:T(8,128)(2,1)} %refs_4_.7) | copy-start | bytes 9437188
  244.9 9.1 %collective-permute-start.1 = (f32[4,25,8,128]{3,2,1,0:T(8,128)S(1)}, f32[4,25,8,128]{3,2,1,0:T(8,128)S(1)}, u32[]{:S(2)}, u32[]{:S(2)}) collective-permute-start(f32[4,25,8,128]{3,2,1,0:T(8,128)S(1)} %get-tuple-element.30), channel_id=1, source_target_pairs={{0,64},{1,193},{2,66},{3,195},{4,68},{5,197},{6,70},{7,199},{8,72}... | collective-permute-start | bytes 1228808 | tf_op jit(solution)/shard_map/ppermute | solution.py:371
  245.5 10.7 %collective-permute-start.12 = (f32[4,25,8,128]{3,2,1,0:T(8,128)S(1)}, f32[4,25,8,128]{3,2,1,0:T(8,128)S(1)}, u32[]{:S(2)}, u32[]{:S(2)}) collective-permute-start(f32[4,25,8,128]{3,2,1,0:T(8,128)S(1)} %get-tuple-element.36), channel_id=1, source_target_pairs={{0,8},{1,57},{2,10},{3,59},{4,12},{5,61},{6,14},{7,63},{8,0},{9,17... | collective-permute-start | bytes 1228808 | tf_op jit(solution)/shard_map/ppermute | solution.py:371
  249.7 10.2 %collective-permute-start = (f32[4,25,8,128]{3,2,1,0:T(8,128)S(1)}, f32[4,25,8,128]{3,2,1,0:T(8,128)S(1)}, u32[]{:S(2)}, u32[]{:S(2)}) collective-permute-start(f32[4,25,8,128]{3,2,1,0:T(8,128)S(1)} %get-tuple-element.28), channel_id=1, source_target_pairs={{0,64},{1,193},{2,66},{3,195},{4,68},{5,197},{6,70},{7,199},{8,72}... | collective-permute-start | bytes 1228808 | tf_op jit(solution)/shard_map/ppermute | solution.py:371
  254.1 8.0 %collective-permute-start.2 = (f32[4,25,8,128]{3,2,1,0:T(8,128)S(1)}, f32[4,25,8,128]{3,2,1,0:T(8,128)S(1)}, u32[]{:S(2)}, u32[]{:S(2)}) collective-permute-start(f32[4,25,8,128]{3,2,1,0:T(8,128)S(1)} %add.2), channel_id=1, source_target_pairs={{0,8},{1,57},{2,10},{3,59},{4,12},{5,61},{6,14},{7,63},{8,0},{9,17... | collective-permute-start | bytes 1228808 | tf_op jit(solution)/shard_map/ppermute | solution.py:371
  254.9 11.6 %collective-permute-start.11 = (f32[4,25,8,128]{3,2,1,0:T(8,128)S(1)}, f32[4,25,8,128]{3,2,1,0:T(8,128)S(1)}, u32[]{:S(2)}, u32[]{:S(2)}) collective-permute-start(f32[4,25,8,128]{3,2,1,0:T(8,128)S(1)} %get-tuple-element.34), channel_id=1, source_target_pairs={{0,8},{1,57},{2,10},{3,59},{4,12},{5,61},{6,14},{7,63},{8,0},{9,17... | collective-permute-start | bytes 1228808 | tf_op jit(solution)/shard_map/ppermute | solution.py:371
  256.2 10.3 %collective-permute-start.13 = (f32[4,25,8,128]{3,2,1,0:T(8,128)S(1)}, f32[4,25,8,128]{3,2,1,0:T(8,128)S(1)}, u32[]{:S(2)}, u32[]{:S(2)}) collective-permute-start(f32[4,25,8,128]{3,2,1,0:T(8,128)S(1)} %add.3), channel_id=1, source_target_pairs={{0,64},{1,193},{2,66},{3,195},{4,68},{5,197},{6,70},{7,199},{8,72}... | collective-permute-start | bytes 1228808 | tf_op jit(solution)/shard_map/ppermute | solution.py:371
  262.2 7.1 %collective-permute-start.3 = (f32[2,25,8,128]{3,2,1,0:T(8,128)S(1)}, f32[2,25,8,128]{3,2,1,0:T(8,128)S(1)}, u32[]{:S(2)}, u32[]{:S(2)}) collective-permute-start(f32[2,25,8,128]{3,2,1,0:T(8,128)S(1)} %get-tuple-element.32), channel_id=1, source_target_pairs={{0,192},{1,65},{2,194},{3,67},{4,196},{5,69},{6,198},{7,71},{8,200... | collective-permute-start | bytes 614408 | tf_op jit(solution)/shard_map/ppermute | solution.py:371
  266.6 7.1 %collective-permute-start.14 = (f32[2,25,8,128]{3,2,1,0:T(8,128)S(1)}, f32[2,25,8,128]{3,2,1,0:T(8,128)S(1)}, u32[]{:S(2)}, u32[]{:S(2)}) collective-permute-start(f32[2,25,8,128]{3,2,1,0:T(8,128)S(1)} %get-tuple-element.38), channel_id=1, source_target_pairs={{0,56},{1,9},{2,58},{3,11},{4,60},{5,13},{6,62},{7,15},{8,16},{9,1... | collective-permute-start | bytes 614408 | tf_op jit(solution)/shard_map/ppermute | solution.py:371
  269.3 6.0 %collective-permute-start.4 = (f32[25,8,128]{2,1,0:T(8,128)S(1)}, f32[25,8,128]{2,1,0:T(8,128)S(1)}, u32[]{:S(2)}, u32[]{:S(2)}) collective-permute-start(f32[25,8,128]{2,1,0:T(8,128)S(1)} %hold.2), channel_id=1, source_target_pairs={{0,56},{1,9},{2,58},{3,11},{4,60},{5,13},{6,62},{7,15},{8,16},{9,1... | collective-permute-start | bytes 307208 | tf_op jit(solution)/shard_map/ppermute | solution.py:371
  273.7 6.0 %collective-permute-start.15 = (f32[25,8,128]{2,1,0:T(8,128)S(1)}, f32[25,8,128]{2,1,0:T(8,128)S(1)}, u32[]{:S(2)}, u32[]{:S(2)}) collective-permute-start(f32[25,8,128]{2,1,0:T(8,128)S(1)} %hold.3), channel_id=1, source_target_pairs={{0,192},{1,65},{2,194},{3,67},{4,196},{5,69},{6,198},{7,71},{8,200... | collective-permute-start | bytes 307208 | tf_op jit(solution)/shard_map/ppermute | solution.py:371
  275.2 9.6 %collective-permute-start.5 = (f32[25,8,128]{2,1,0:T(8,128)S(1)}, f32[25,8,128]{2,1,0:T(8,128)S(1)}, u32[]{:S(2)}, u32[]{:S(2)}) collective-permute-start(f32[25,8,128]{2,1,0:T(8,128)S(1)} %own.2.sum_ref), channel_id=1, source_target_pairs={{0,24},{1,41},{2,26},{3,43},{4,28},{5,45},{6,30},{7,47},{8,48},{9,... | collective-permute-start | bytes 307208 | tf_op jit(solution)/shard_map/ppermute | solution.py:371
  279.6 7.2 %collective-permute-start.16 = (f32[25,8,128]{2,1,0:T(8,128)S(1)}, f32[25,8,128]{2,1,0:T(8,128)S(1)}, u32[]{:S(2)}, u32[]{:S(2)}) collective-permute-start(f32[25,8,128]{2,1,0:T(8,128)S(1)} %own.3.sum_ref), channel_id=1, source_target_pairs={{0,24},{1,41},{2,26},{3,43},{4,28},{5,45},{6,30},{7,47},{8,48},{9,... | collective-permute-start | bytes 307208 | tf_op jit(solution)/shard_map/ppermute | solution.py:371
  285.0 5.9 %collective-permute-start.6 = (f32[32,768]{1,0:T(8,128)S(1)}, f32[32,768]{1,0:T(8,128)S(1)}, u32[]{:S(2)}, u32[]{:S(2)}) collective-permute-start(f32[32,768]{1,0:T(8,128)S(1)} %mean.2.refs_3_), channel_id=1, source_target_pairs={{0,56},{1,9},{2,58},{3,11},{4,60},{5,13},{6,62},{7,15},{8,16},{9,1... | collective-permute-start | bytes 294920 | tf_op jit(solution)/shard_map/ppermute | solution.py:371
  286.9 7.1 %collective-permute-start.17 = (f32[32,768]{1,0:T(8,128)S(1)}, f32[32,768]{1,0:T(8,128)S(1)}, u32[]{:S(2)}, u32[]{:S(2)}) collective-permute-start(f32[32,768]{1,0:T(8,128)S(1)} %mean.3.refs_3_), channel_id=1, source_target_pairs={{0,192},{1,65},{2,194},{3,67},{4,196},{5,69},{6,198},{7,71},{8,200... | collective-permute-start | bytes 294920 | tf_op jit(solution)/shard_map/ppermute | solution.py:371
  289.0 7.5 %collective-permute-start.8 = (f32[32,768]{1,0:T(8,128)S(1)}, f32[32,768]{1,0:T(8,128)S(1)}, u32[]{:S(2)}, u32[]{:S(2)}) collective-permute-start(f32[32,768]{1,0:T(8,128)S(1)} %mean.2.refs_3_), channel_id=1, source_target_pairs={{0,192},{1,65},{2,194},{3,67},{4,196},{5,69},{6,198},{7,71},{8,200... | collective-permute-start | bytes 294920 | tf_op jit(solution)/shard_map/ppermute | solution.py:371
  290.9 6.9 %collective-permute-start.7 = (f32[32,768]{1,0:T(8,128)S(1)}, f32[32,768]{1,0:T(8,128)S(1)}, u32[]{:S(2)}, u32[]{:S(2)}) collective-permute-start(f32[32,768]{1,0:T(8,128)S(1)} %collective-permute-done.6.refs_2_), channel_id=1, source_target_pairs={{0,192},{1,65},{2,194},{3,67},{4,196},{5,69},{6,198},{7,71},{8,200... | collective-permute-start | bytes 294920 | tf_op jit(solution)/shard_map/ppermute | solution.py:371
  293.2 6.7 %collective-permute-start.19 = (f32[32,768]{1,0:T(8,128)S(1)}, f32[32,768]{1,0:T(8,128)S(1)}, u32[]{:S(2)}, u32[]{:S(2)}) collective-permute-start(f32[32,768]{1,0:T(8,128)S(1)} %mean.3.refs_3_), channel_id=1, source_target_pairs={{0,56},{1,9},{2,58},{3,11},{4,60},{5,13},{6,62},{7,15},{8,16},{9,1... | collective-permute-start | bytes 294920 | tf_op jit(solution)/shard_map/ppermute | solution.py:371
  294.0 8.0 %collective-permute-start.18 = (f32[32,768]{1,0:T(8,128)S(1)}, f32[32,768]{1,0:T(8,128)S(1)}, u32[]{:S(2)}, u32[]{:S(2)}) collective-permute-start(f32[32,768]{1,0:T(8,128)S(1)} %collective-permute-done.17.refs_2_), channel_id=1, source_target_pairs={{0,56},{1,9},{2,58},{3,11},{4,60},{5,13},{6,62},{7,15},{8,16},{9,1... | collective-permute-start | bytes 294920 | tf_op jit(solution)/shard_map/ppermute | solution.py:371
  297.8 7.9 %collective-permute-start.9 = (f32[128,768]{1,0:T(8,128)S(1)}, f32[128,768]{1,0:T(8,128)S(1)}, u32[]{:S(2)}, u32[]{:S(2)}) collective-permute-start(f32[128,768]{1,0:T(8,128)S(1)} %join.2.refs_0_), channel_id=1, source_target_pairs={{0,8},{1,57},{2,10},{3,59},{4,12},{5,61},{6,14},{7,63},{8,0},{9,17... | collective-permute-start | bytes 1179656 | tf_op jit(solution)/shard_map/ppermute | solution.py:371
  302.1 7.9 %collective-permute-start.20 = (f32[128,768]{1,0:T(8,128)S(1)}, f32[128,768]{1,0:T(8,128)S(1)}, u32[]{:S(2)}, u32[]{:S(2)}) collective-permute-start(f32[128,768]{1,0:T(8,128)S(1)} %join.3.refs_1_), channel_id=1, source_target_pairs={{0,64},{1,193},{2,66},{3,195},{4,68},{5,197},{6,70},{7,199},{8,72}... | collective-permute-start | bytes 1179656 | tf_op jit(solution)/shard_map/ppermute | solution.py:371
  302.2 12.0 %collective-permute-start.22 = (f32[128,768]{1,0:T(8,128)S(1)}, f32[128,768]{1,0:T(8,128)S(1)}, u32[]{:S(2)}, u32[]{:S(2)}) collective-permute-start(f32[128,768]{1,0:T(8,128)S(1)} %join.2.refs_0_), channel_id=1, source_target_pairs={{0,64},{1,193},{2,66},{3,195},{4,68},{5,197},{6,70},{7,199},{8,72}... | collective-permute-start | bytes 1179656 | tf_op jit(solution)/shard_map/ppermute | solution.py:371
  304.2 10.0 %collective-permute-start.23 = (f32[128,768]{1,0:T(8,128)S(1)}, f32[128,768]{1,0:T(8,128)S(1)}, u32[]{:S(2)}, u32[]{:S(2)}) collective-permute-start(f32[128,768]{1,0:T(8,128)S(1)} %join.3.refs_1_), channel_id=1, source_target_pairs={{0,8},{1,57},{2,10},{3,59},{4,12},{5,61},{6,14},{7,63},{8,0},{9,17... | collective-permute-start | bytes 1179656 | tf_op jit(solution)/shard_map/ppermute | solution.py:371
  305.7 12.7 %collective-permute-start.10 = (f32[128,768]{1,0:T(8,128)S(1)}, f32[128,768]{1,0:T(8,128)S(1)}, u32[]{:S(2)}, u32[]{:S(2)}) collective-permute-start(f32[128,768]{1,0:T(8,128)S(1)} %collective-permute-done.9.refs_2_), channel_id=1, source_target_pairs={{0,64},{1,193},{2,66},{3,195},{4,68},{5,197},{6,70},{7,199},{8,72}... | collective-permute-start | bytes 1179656 | tf_op jit(solution)/shard_map/ppermute | solution.py:371
  309.9 8.4 %collective-permute-start.21 = (f32[128,768]{1,0:T(8,128)S(1)}, f32[128,768]{1,0:T(8,128)S(1)}, u32[]{:S(2)}, u32[]{:S(2)}) collective-permute-start(f32[128,768]{1,0:T(8,128)S(1)} %collective-permute-done.20.refs_3_), channel_id=1, source_target_pairs={{0,8},{1,57},{2,10},{3,59},{4,12},{5,61},{6,14},{7,63},{8,0},{9,17... | collective-permute-start | bytes 1179656 | tf_op jit(solution)/shard_map/ppermute | solution.py:371
